TPU v7x, 32 devices: a whole 2x2x4 slice. The times are simulated.
32 devices in a mesh: dp: 16 (over z, x, core), own: 2 (over y).
Axes of the slice: x: 2, y: 2, z: 4, core: 2. Of those that a mesh axis runs over, the one named last changes fastest.
Arguments:
- latents: bfloat16 [64, 1024, 384], P(('dp', 'own')), may hold values from -6 to 6
- condition: bfloat16 [64, 384], P(('dp', 'own')), may hold values from -6 to 6
- cotangent: bfloat16 [64, 1024, 384], P(('dp', 'own')), may hold values from -6 to 6
- owner: int32 [18], replicated, may hold values from 0 to 1, as said below
- master: float32 [20, 384, 384], P('own')
- stat_left: float32 [20, 384, 384], P('own'), as said below
- stat_right: float32 [20, 384, 384], P('own'), as said below
- root_left: float32 [20, 384, 384], P('own'), as said below
- root_right: float32 [20, 384, 384], P('own'), as said below
- bias: float32 [5760], replicated, may hold values from -1.2 to 1.2
- moment_one: float32 [5760], replicated, may hold values from -51.2 to 51.2
- moment_two: float32 [5760], replicated, may hold values from 308.0192 to 1245.184
Outputs:
- block_out: bfloat16 [64, 1024, 384], P(('dp', 'own'))
- latents_grad: float32 [64, 1024, 384], P(('dp', 'own'))
- condition_grad: float32 [64, 384], P(('dp', 'own'))
- weight_grads: float32 [20, 384, 384], P('own')
- stat_left_new: float32 [20, 384, 384], P('own')
- stat_right_new: float32 [20, 384, 384], P('own')
- master_new: float32 [20, 384, 384], P('own')
- bias_grad: float32 [5760], replicated
- moment_one_new: float32 [5760], replicated
- moment_two_new: float32 [5760], replicated
- bias_new: float32 [5760], replicated
Inputs may be any that keep to these rules, and one draw needn't show every extreme that they name: owner[b] is the device along own that keeps block b; no device keeps more than 10 blocks, and some device keeps exactly 10. `stat_left`: each matrix is symmetric. `stat_right`: each matrix is symmetric. `root_left`: each matrix is symmetric. `root_right`: each matrix is symmetric.
All inputs are finite; a program needn't handle non-finite values.
Results may differ from a plain program's by a relative error of at most 0.015.
The roundings to bfloat16 on the way count: a program that leaves them out, or rounds other values in their place, can miss the bound.
Values may be sent and summed in bfloat16 or wider, within the bound.
No kernel may reach another device: no remote copies, remote signals or barrier semaphores. Data moves between devices by JAX's collectives and lax.ppermute only.
A program may use at most 256 MiB of HBM per device.

v0:
```python
import jax
import jax.numpy as jnp
from jax import lax
from jax.sharding import PartitionSpec as P

D = 384
H = 6
HD = 64
FF = 1536
QBLOCK = 512
STEP = 10


highest = lax.Precision.HIGHEST
norm_eps = 1e-06
shampoo_rate = 1.0
shampoo_decay = 0.01
adam_rate = 0.2
adam_decay = 0.01


def product(left_side, right_side):
    return jnp.dot(left_side, right_side, preferred_element_type=jnp.float32)


def contract_rows(left_side, right_side):
    return lax.dot_general(
        left_side, right_side, (((0,), (0,)), ((), ())), preferred_element_type=jnp.float32
    )


def times_transpose(left_side, right_side):
    return lax.dot_general(
        left_side, right_side, (((1,), (1,)), ((), ())), preferred_element_type=jnp.float32
    )


def slot_places(owner, slot_count):
    order = jnp.arange(owner.shape[0], dtype=jnp.int32)
    before = (order[None, :] < order[:, None]) & (owner[None, :] == owner[:, None])
    return owner * slot_count + jnp.sum(before.astype(jnp.int32), axis=1)


def column_blocks(blocks):
    return jnp.transpose(blocks, (1, 0, 2)).reshape(
        blocks.shape[1], blocks.shape[0] * blocks.shape[2]
    )


def split_columns(matrix, count):
    return jnp.transpose(matrix.reshape(matrix.shape[0], count, matrix.shape[0]), (1, 0, 2))


def layer_norm(value):
    centered = value - jnp.mean(value, axis=-1, keepdims=True)
    inverse = lax.rsqrt(jnp.mean(centered * centered, axis=-1, keepdims=True) + norm_eps)
    return (centered * inverse, inverse)


def norm_back(gradient, normed, inverse):
    return inverse * (
        gradient
        - jnp.mean(gradient, axis=-1, keepdims=True)
        - normed * jnp.mean(gradient * normed, axis=-1, keepdims=True)
    )


def attend(entries):
    query, keys, values = entries
    score_scale = HD ** (-0.5)
    outputs = []
    totals = []
    for offset in range(0, query.shape[0], QBLOCK):
        block_rows = query[offset : offset + QBLOCK]
        scores = (
            jnp.einsum("qhd,khd->hqk", block_rows, keys, preferred_element_type=jnp.float32)
            * score_scale
        )
        row_peak = jnp.max(scores, axis=-1, keepdims=True)
        expo_scores = jnp.exp(scores - row_peak)
        row_total = jnp.sum(expo_scores, axis=-1, keepdims=True)
        probabilities = (expo_scores / row_total).astype(jnp.bfloat16)
        outputs.append(
            jnp.einsum(
                "hqk,khd->qhd", probabilities, values, preferred_element_type=jnp.float32
            ).astype(jnp.bfloat16)
        )
        totals.append(row_peak + jnp.log(row_total))
    return (jnp.concatenate(outputs, axis=0), jnp.concatenate(totals, axis=1))


def attend_back(entries):
    query, keys, values, back_out, totals = entries
    score_scale = HD ** (-0.5)
    back_keys = jnp.zeros(keys.shape, jnp.float32)
    back_values = jnp.zeros(values.shape, jnp.float32)
    back_queries = []
    for offset in range(0, query.shape[0], QBLOCK):
        block_rows = query[offset : offset + QBLOCK]
        back_rows = back_out[offset : offset + QBLOCK]
        scores = (
            jnp.einsum("qhd,khd->hqk", block_rows, keys, preferred_element_type=jnp.float32)
            * score_scale
        )
        probabilities = jnp.exp(scores - totals[:, offset : offset + QBLOCK])
        back_probs = jnp.einsum(
            "qhd,khd->hqk", back_rows, values, preferred_element_type=jnp.float32
        )
        back_values = back_values + jnp.einsum(
            "hqk,qhd->khd",
            probabilities.astype(jnp.bfloat16),
            back_rows,
            preferred_element_type=jnp.float32,
        )
        row_delta = jnp.sum(probabilities * back_probs, axis=-1, keepdims=True)
        back_scores = (probabilities * (back_probs - row_delta) * score_scale).astype(jnp.bfloat16)
        back_queries.append(
            jnp.einsum("hqk,khd->qhd", back_scores, keys, preferred_element_type=jnp.float32)
        )
        back_keys = back_keys + jnp.einsum(
            "hqk,qhd->khd", back_scores, block_rows, preferred_element_type=jnp.float32
        )
    back_query = jnp.concatenate(back_queries, axis=0)
    return jnp.stack([back_query, back_keys, back_values], axis=1).astype(jnp.bfloat16)


def per_device(
    latents,
    condition,
    cotangent,
    owner,
    master,
    stat_left,
    stat_right,
    root_left,
    root_right,
    bias,
    moment_one,
    moment_two,
):
    slot_count = master.shape[0]
    seq_count = latents.shape[0]
    seq_length = latents.shape[1]
    tokens = seq_count * seq_length
    ffn_blocks = FF // D
    places = slot_places(owner, slot_count)
    gathered = lax.all_gather(master.astype(jnp.bfloat16), "own", axis=0, tiled=True)
    weights = gathered[places]
    weight_qkv = column_blocks(weights[0:3])
    weight_proj = weights[3]
    weight_up = column_blocks(weights[4 : 4 + ffn_blocks])
    weight_down = weights[4 + ffn_blocks : 4 + 2 * ffn_blocks].reshape(FF, D)
    weight_ada = column_blocks(weights[4 + 2 * ffn_blocks :])
    bias_qkv = bias[0 : 3 * D]
    bias_proj = bias[3 * D : 4 * D]
    bias_up = bias[4 * D : 4 * D + FF]
    bias_down = bias[4 * D + FF : 5 * D + FF]
    bias_ada = bias[5 * D + FF :]
    cond_float = condition.astype(jnp.float32)
    silu_cond, silu_pull = jax.vjp(jax.nn.silu, cond_float)
    cond_low = silu_cond.astype(jnp.bfloat16)
    modulation = product(cond_low, weight_ada) + bias_ada
    pieces = [modulation[:, None, j * D : (j + 1) * D] for j in range(6)]
    shift_one, scale_one, gate_one, shift_two, scale_two, gate_two = pieces
    latent_float = latents.astype(jnp.float32)
    norm_one, inverse_one = layer_norm(latent_float)
    first_in = (norm_one * (1.0 + scale_one) + shift_one).astype(jnp.bfloat16).reshape(tokens, D)
    qkv_low = (
        (product(first_in, weight_qkv) + bias_qkv)
        .astype(jnp.bfloat16)
        .reshape(seq_count, seq_length, 3, H, HD)
    )
    query = qkv_low[:, :, 0]
    keys = qkv_low[:, :, 1]
    values = qkv_low[:, :, 2]
    attn_mixed, totals = lax.map(attend, (query, keys, values))
    mixed_flat = attn_mixed.reshape(tokens, D)
    attn_out = (product(mixed_flat, weight_proj) + bias_proj).reshape(seq_count, seq_length, D)
    residual = latent_float + gate_one * attn_out
    norm_two, inverse_two = layer_norm(residual)
    second_in = (norm_two * (1.0 + scale_two) + shift_two).astype(jnp.bfloat16).reshape(tokens, D)
    hidden_pre = product(second_in, weight_up) + bias_up
    hidden_float, gelu_pull = jax.vjp(
        lambda value: jax.nn.gelu(value, approximate=True), hidden_pre
    )
    hidden_act = hidden_float.astype(jnp.bfloat16)
    ffn_out = (product(hidden_act, weight_down) + bias_down).reshape(seq_count, seq_length, D)
    block_out = (residual + gate_two * ffn_out).astype(jnp.bfloat16)
    upstream = cotangent.astype(jnp.float32)
    back_ffn = (upstream * gate_two).astype(jnp.bfloat16).reshape(tokens, D)
    back_gate_two = jnp.sum(upstream * ffn_out, axis=1)
    grad_down = contract_rows(hidden_act, back_ffn)
    back_act = times_transpose(back_ffn, weight_down)
    back_pre = gelu_pull(back_act)[0].astype(jnp.bfloat16)
    grad_up = contract_rows(second_in, back_pre)
    back_second = times_transpose(back_pre, weight_up).reshape(seq_count, seq_length, D)
    back_scale_two = jnp.sum(back_second * norm_two, axis=1)
    back_shift_two = jnp.sum(back_second, axis=1)
    back_residual = upstream + norm_back(back_second * (1.0 + scale_two), norm_two, inverse_two)
    back_attn = (back_residual * gate_one).astype(jnp.bfloat16).reshape(tokens, D)
    back_gate_one = jnp.sum(back_residual * attn_out, axis=1)
    grad_proj = contract_rows(mixed_flat, back_attn)
    back_mixed = (
        times_transpose(back_attn, weight_proj)
        .astype(jnp.bfloat16)
        .reshape(seq_count, seq_length, H, HD)
    )
    back_qkv = lax.map(attend_back, (query, keys, values, back_mixed, totals))
    back_qkv_flat = back_qkv.reshape(tokens, 3 * D)
    grad_qkv = contract_rows(first_in, back_qkv_flat)
    back_first = times_transpose(back_qkv_flat, weight_qkv).reshape(seq_count, seq_length, D)
    back_scale_one = jnp.sum(back_first * norm_one, axis=1)
    back_shift_one = jnp.sum(back_first, axis=1)
    latents_grad = back_residual + norm_back(back_first * (1.0 + scale_one), norm_one, inverse_one)
    back_mod = jnp.concatenate(
        [
            back_shift_one,
            back_scale_one,
            back_gate_one,
            back_shift_two,
            back_scale_two,
            back_gate_two,
        ],
        axis=-1,
    ).astype(jnp.bfloat16)
    grad_ada = contract_rows(cond_low, back_mod)
    condition_grad = silu_pull(times_transpose(back_mod, weight_ada))[0]
    block_grads = jnp.concatenate(
        [
            split_columns(grad_qkv, 3),
            grad_proj[None],
            split_columns(grad_up, ffn_blocks),
            grad_down.reshape(ffn_blocks, D, D),
            split_columns(grad_ada, 6),
        ],
        axis=0,
    )
    bias_grads = jnp.concatenate(
        [
            jnp.sum(back_qkv_flat, axis=0, dtype=jnp.float32),
            jnp.sum(back_attn, axis=0, dtype=jnp.float32),
            jnp.sum(back_pre, axis=0, dtype=jnp.float32),
            jnp.sum(back_ffn, axis=0, dtype=jnp.float32),
            jnp.sum(back_mod, axis=0, dtype=jnp.float32),
        ]
    )
    total_slots = slot_count * lax.axis_size("own")
    summed = lax.psum(block_grads, "dp")
    owned_grads = lax.psum_scatter(
        jnp.zeros((total_slots, D, D), jnp.float32).at[places].set(summed),
        "own",
        scatter_dimension=0,
        tiled=True,
    )
    bias_grad = lax.psum(bias_grads, ("dp", "own"))
    member = lax.axis_index("own")
    filled = jnp.sum((owner == member).astype(jnp.int32))

    def occupied(gradient, left_stat, right_stat, left_root, right_root, weight):
        left_new = 0.5 * left_stat + 0.5 * jnp.dot(gradient, gradient.T, precision=highest)
        right_new = 0.5 * right_stat + 0.5 * jnp.dot(gradient.T, gradient, precision=highest)
        direction = jnp.dot(
            jnp.dot(left_root, gradient, precision=highest), right_root, precision=highest
        )
        scaled = (
            jnp.sqrt(jnp.mean(weight * weight) + norm_eps)
            * direction
            * lax.rsqrt(jnp.mean(direction * direction) + norm_eps)
        )
        return (left_new, right_new, weight - shampoo_rate * (scaled + shampoo_decay * weight))

    def vacant(gradient, left_stat, right_stat, left_root, right_root, weight):
        return (0.5 * left_stat, 0.5 * right_stat, weight - shampoo_rate * (shampoo_decay * weight))

    def renew(entries):
        slot_index, gradient, left_stat, right_stat, left_root, right_root, weight = entries
        return lax.cond(
            slot_index < filled,
            occupied,
            vacant,
            gradient,
            left_stat,
            right_stat,
            left_root,
            right_root,
            weight,
        )

    stat_left_new, stat_right_new, master_new = lax.map(
        renew,
        (
            jnp.arange(slot_count, dtype=jnp.int32),
            owned_grads,
            stat_left,
            stat_right,
            root_left,
            root_right,
            master,
        ),
    )
    moment_one_new = 0.9 * moment_one + 0.1 * bias_grad
    moment_two_new = 0.95 * moment_two + 0.05 * bias_grad * bias_grad
    corrected = (
        moment_one_new / (1.0 - 0.9**STEP) / (jnp.sqrt(moment_two_new / (1.0 - 0.95**STEP)) + 1e-08)
    )
    bias_new = bias - adam_rate * (corrected + adam_decay * bias)
    return (
        block_out,
        latents_grad,
        condition_grad,
        owned_grads,
        stat_left_new,
        stat_right_new,
        master_new,
        bias_grad,
        moment_one_new,
        moment_two_new,
        bias_new,
    )


def solution(mesh):
    placed = (
        P(("dp", "own"), None, None),
        P(("dp", "own"), None),
        P(("dp", "own"), None, None),
        P(),
        P("own", None, None),
        P("own", None, None),
        P("own", None, None),
        P("own", None, None),
        P("own", None, None),
        P(),
        P(),
        P(),
    )
    return jax.shard_map(
        per_device,
        mesh=mesh,
        in_specs=placed,
        out_specs=(
            P(("dp", "own"), None, None),
            P(("dp", "own"), None, None),
            P(("dp", "own"), None),
            P("own", None, None),
            P("own", None, None),
            P("own", None, None),
            P("own", None, None),
            P(),
            P(),
            P(),
            P(),
        ),
        check_vma=False,
    )
```

profile of v0, /device:TPU:0, one launch (start us, length us, event | category | flops | bytes accessed | tf_op | source)
XLA Modules:
  0.0 1233.7 jit_solution(13551716028039895665)
XLA Ops:
  16.0 74.9 %all-gather.2.cloned.1.call-done = bf16[20,384,384]{2,1,0:T(8,128)(2,1)} async-done(((bf16[10,384,384]{2,1,0:T(8,128)(2,1)}), bf16[20,384,384]{2,1,0:T(8,128)(2,1)}) %all-gather.2.cloned.1.call-update) | async-done | bytes 5898256 | tf_op jit(solution)/shard_map/all_gather | solution.py:147
  152.5 41.6 %while.36 = (s32[]{:T(128)}, bf16[2,1024,6,64]{1,3,2,0:T(8,128)(2,1)S(1)}, f32[2,6,1024,1]{2,1,3,0:T(8,128)}, bf16[2,1024,6,64]{1,3,2,0:T(8,128)(2,1)}, bf16[2,1...) while((s32[]{:T(128)}, ...), condition=%wide.region_8.9_spmd, body=%wide.region_3.8_spmd.sunk | while | flops 1669201920 | bytes 82045568 | solution.py:176
  206.0 17.0 %convert_reduce_fusion = (f32[1536]{0:T(1024)}, bf16[2048,1536]{0,1:T(8,128)(2,1)}, f32[2048,1536]{0,1:T(8,128)}) fusion(f32[2048,1536]{0,1:T(8,128)S(1)} %fusion.212, f32[1536]{0:T(1024)S(1)} %copy-done.46, bf16[2048,384]{1,0:T(8,128)(2,1)S(1)} %bitcast.341, bf16[384,1536]{1,0:T(8,128)(2,1)} %bitcast.345), kind=kOutput, calls=%fused_computation.176 | convolution fusion | flops 2488269312 | bytes 34222080 | tf_op jit(solution)/shard_map/dot_general | solution.py:23
  286.3 316.6 %while.37 = (s32[]{:T(128)}, bf16[2,1024,3,6,64]{1,4,3,2,0:T(8,128)(2,1)}, bf16[2,1024,6,64]{1,3,2,0:T(8,128)(2,1)S(1)}, bf16[2,1024,6,64]{1,3,2,0:T(8,128)(2,1)...) while((s32[]{:T(128)}, ...), condition=%wide.region_16.17_spmd, body=%wide.region_13.16_spmd.sunk | while | flops 4169285632 | bytes 400553152 | solution.py:208
  313.1 32.9 %fusion.298 = bf16[512,6,64]{0,2,1:T(8,128)(2,1)S(1)} fusion(f32[6,512,1024]{2,1,0:T(8,128)} %fusion.293, f32[6,512,1024]{2,1,0:T(8,128)} %copy-done.1, f32[6,512]{1,0:T(8,128)S(1)} %get-tuple-element.589, bf16[2,1024,6,64]{1,3,2,0:T(8,128)(2,1)S(1)} %get-tuple-element.665, s32[]{:T(128)S(6)} %copy.184), kind=kOutput, calls=%fused_computation.77.clone.1 | convolution fusion | flops 431165440 | bytes 51544068 | tf_op jit(solution)/shard_map/while/body/eval_jaxpr/hqk,khd->qhd/dot_general | solution.py:118
  346.0 27.7 %fusion.294 = f32[6,64,1024]{2,1,0:T(8,128)} fusion(f32[6,512,1024]{2,1,0:T(8,128)} %fusion.293, f32[6,512,1024]{2,1,0:T(8,128)} %copy-done.1, f32[6,512]{1,0:T(8,128)S(1)} %get-tuple-element.589, bf16[2,1024,6,64]{1,3,2,0:T(8,128)(2,1)} %get-tuple-element.666, s32[]{:T(128)S(6)} %copy.184), kind=kOutput, calls=%fused_computation.51.clone.1 | convolution fusion | flops 430968832 | bytes 52330500 | tf_op jit(solution)/shard_map/while/body/eval_jaxpr/hqk,qhd->khd/dot_general | solution.py:120
  381.2 27.0 %fusion.296 = bf16[1,1024,1,6,64]{1,4,3,2,0:T(8,128)(2,1)S(1)} fusion(f32[6,64,1024]{2,1,0:T(8,128)} %fusion.294, f32[6,512,1024]{2,1,0:T(8,128)} %fusion.295, f32[6,512,1024]{2,1,0:T(8,128)} %copy-done, f32[6,512]{1,0:T(8,128)S(1)} %get-tuple-element.588, bf16[2,1024,6,64]{1,3,2,0:T(8,128)(2,1)} %get-tuple-element.666, s32[]{:T(128)S(6)} %copy.184, ...), kind=kOutput, calls=%fused_computation.73.clone.1 | convolution fusion | flops 431755264 | bytes 53116936 | tf_op jit(solution)/shard_map/while/body/eval_jaxpr/hqk,qhd->khd/dot_general | solution.py:120
  408.2 33.5 %fusion.297 = bf16[512,6,64]{0,2,1:T(8,128)(2,1)} fusion(f32[6,512,1024]{2,1,0:T(8,128)} %fusion.295, f32[6,512,1024]{2,1,0:T(8,128)} %copy-done, f32[6,512]{1,0:T(8,128)S(1)} %get-tuple-element.588, bf16[2,1024,6,64]{1,3,2,0:T(8,128)(2,1)S(1)} %get-tuple-element.665, s32[]{:T(128)S(6)} %copy.184), kind=kOutput, calls=%fused_computation.78.clone.1 | convolution fusion | flops 431165440 | bytes 51544068 | tf_op jit(solution)/shard_map/while/body/eval_jaxpr/hqk,khd->qhd/dot_general | solution.py:118
  471.2 32.9 %fusion.298 = bf16[512,6,64]{0,2,1:T(8,128)(2,1)S(1)} fusion(f32[6,512,1024]{2,1,0:T(8,128)} %fusion.293, f32[6,512,1024]{2,1,0:T(8,128)} %copy-done.1, f32[6,512]{1,0:T(8,128)S(1)} %get-tuple-element.589, bf16[2,1024,6,64]{1,3,2,0:T(8,128)(2,1)S(1)} %get-tuple-element.665, s32[]{:T(128)S(6)} %copy.184), kind=kOutput, calls=%fused_computation.77.clone.1 | convolution fusion | flops 431165440 | bytes 51544068 | tf_op jit(solution)/shard_map/while/body/eval_jaxpr/hqk,khd->qhd/dot_general | solution.py:118
  504.0 27.6 %fusion.294 = f32[6,64,1024]{2,1,0:T(8,128)} fusion(f32[6,512,1024]{2,1,0:T(8,128)} %fusion.293, f32[6,512,1024]{2,1,0:T(8,128)} %copy-done.1, f32[6,512]{1,0:T(8,128)S(1)} %get-tuple-element.589, bf16[2,1024,6,64]{1,3,2,0:T(8,128)(2,1)} %get-tuple-element.666, s32[]{:T(128)S(6)} %copy.184), kind=kOutput, calls=%fused_computation.51.clone.1 | convolution fusion | flops 430968832 | bytes 52330500 | tf_op jit(solution)/shard_map/while/body/eval_jaxpr/hqk,qhd->khd/dot_general | solution.py:120
  539.2 27.0 %fusion.296 = bf16[1,1024,1,6,64]{1,4,3,2,0:T(8,128)(2,1)S(1)} fusion(f32[6,64,1024]{2,1,0:T(8,128)} %fusion.294, f32[6,512,1024]{2,1,0:T(8,128)} %fusion.295, f32[6,512,1024]{2,1,0:T(8,128)} %copy-done, f32[6,512]{1,0:T(8,128)S(1)} %get-tuple-element.588, bf16[2,1024,6,64]{1,3,2,0:T(8,128)(2,1)} %get-tuple-element.666, s32[]{:T(128)S(6)} %copy.184, ...), kind=kOutput, calls=%fused_computation.73.clone.1 | convolution fusion | flops 431755264 | bytes 53116936 | tf_op jit(solution)/shard_map/while/body/eval_jaxpr/hqk,qhd->khd/dot_general | solution.py:120
  566.2 33.5 %fusion.297 = bf16[512,6,64]{0,2,1:T(8,128)(2,1)} fusion(f32[6,512,1024]{2,1,0:T(8,128)} %fusion.295, f32[6,512,1024]{2,1,0:T(8,128)} %copy-done, f32[6,512]{1,0:T(8,128)S(1)} %get-tuple-element.588, bf16[2,1024,6,64]{1,3,2,0:T(8,128)(2,1)S(1)} %get-tuple-element.665, s32[]{:T(128)S(6)} %copy.184), kind=kOutput, calls=%fused_computation.78.clone.1 | convolution fusion | flops 431165440 | bytes 51544068 | tf_op jit(solution)/shard_map/while/body/eval_jaxpr/hqk,khd->qhd/dot_general | solution.py:118
  647.8 202.6 %all-reduce.2.cloned.1.call-done = f32[18,384,384]{1,2,0:T(8,128)} async-done(((f32[18,384,384]{1,2,0:T(8,128)}), f32[18,384,384]{1,2,0:T(8,128)}) %all-reduce.2.cloned.1.call-update) | async-done | bytes 10616848 | tf_op jit(solution)/shard_map/psum | solution.py:248
  868.8 19.6 %scatter_fusion = f32[20,384,384]{2,1,0:T(8,128)} fusion(f32[20,384,384]{2,1,0:T(8,128)} %broadcast_in_dim.38, s32[18]{0:T(128)S(1)} %copy-done.51, f32[18,384,384]{2,1,0:T(8,128)} %copy.146), kind=kCustom, calls=%fused_computation.1 | custom fusion | bytes 31850568 | tf_op jit(solution)/shard_map/scatter | solution.py:250
  891.9 41.1 %psum.15 = f32[5760]{0:T(1024)S(1)} all-reduce(f32[5760]{0:T(1024)S(1)} %constant_dynamic-update-slice_fusion.12), channel_id=1, replica_groups=mesh['dp'=16,'own'=2] {'dp','own'}, use_global_device_ids=true, to_apply=%region_40.41 | all-reduce | flops 5760 | bytes 46080 | tf_op jit(solution)/shard_map/psum | solution.py:255
  934.6 91.6 %reduce-scatter.2.cloned.1.call-done = f32[10,384,384]{2,1,0:T(8,128)} async-done(((f32[20,384,384]{2,1,0:T(8,128)}), f32[10,384,384]{2,1,0:T(8,128)}) %reduce-scatter.2.cloned.1.call-update) | async-done | bytes 5898256 | tf_op jit(solution)/shard_map/reduce_scatter | solution.py:249
  1026.2 200.7 %while.38 = (s32[]{:T(128)}, f32[10,384,384]{2,1,0:T(8,128)}, f32[10,384,384]{2,1,0:T(8,128)}, f32[10,384,384]{2,1,0:T(8,128)}, s32[10]{0:T(128)S(1)}, /*index=5...) while((s32[]{:T(128)}, f32[10,384,384]{2,1,0:T(8,128)}, ...), condition=%wide.region_34.35_spmd, body=%wide.region_29.34_spmd.sunk | while | flops 2719825920 | bytes 17108844 | solution.py:289
  1031.2 13.1 %conditional.2 = (f32[384,384]{1,0:T(8,128)S(1)}, f32[384,384]{1,0:T(8,128)S(1)}, f32[384,384]{1,0:T(8,128)S(1)}, f32[384,384]{1,0:T(8,128)S(1)}) conditional(s32[]{:T(128)} %convert_element_type.301, (f32[384,384]{1,0:T(8,128)S(1)}, f32[384,384]{1,0:T(8,128)S(1)}, f32[384,384]{1,0:T(8,128)S(1)}) %tuple.132, (f32[10,384,384]{2,1,0:T(8,128)}, ...), branch_computations={%region_30.30_spmd, %region_31.33_spmd} | conditional | flops 2719383552 | bytes 9439856 | solution.py:277
  1051.3 13.1 %conditional.2 = (f32[384,384]{1,0:T(8,128)S(1)}, f32[384,384]{1,0:T(8,128)S(1)}, f32[384,384]{1,0:T(8,128)S(1)}, f32[384,384]{1,0:T(8,128)S(1)}) conditional(s32[]{:T(128)} %convert_element_type.301, (f32[384,384]{1,0:T(8,128)S(1)}, f32[384,384]{1,0:T(8,128)S(1)}, f32[384,384]{1,0:T(8,128)S(1)}) %tuple.132, (f32[10,384,384]{2,1,0:T(8,128)}, ...), branch_computations={%region_30.30_spmd, %region_31.33_spmd} | conditional | flops 2719383552 | bytes 9439856 | solution.py:277
  1071.3 13.1 %conditional.2 = (f32[384,384]{1,0:T(8,128)S(1)}, f32[384,384]{1,0:T(8,128)S(1)}, f32[384,384]{1,0:T(8,128)S(1)}, f32[384,384]{1,0:T(8,128)S(1)}) conditional(s32[]{:T(128)} %convert_element_type.301, (f32[384,384]{1,0:T(8,128)S(1)}, f32[384,384]{1,0:T(8,128)S(1)}, f32[384,384]{1,0:T(8,128)S(1)}) %tuple.132, (f32[10,384,384]{2,1,0:T(8,128)}, ...), branch_computations={%region_30.30_spmd, %region_31.33_spmd} | conditional | flops 2719383552 | bytes 9439856 | solution.py:277
  1091.4 13.1 %conditional.2 = (f32[384,384]{1,0:T(8,128)S(1)}, f32[384,384]{1,0:T(8,128)S(1)}, f32[384,384]{1,0:T(8,128)S(1)}, f32[384,384]{1,0:T(8,128)S(1)}) conditional(s32[]{:T(128)} %convert_element_type.301, (f32[384,384]{1,0:T(8,128)S(1)}, f32[384,384]{1,0:T(8,128)S(1)}, f32[384,384]{1,0:T(8,128)S(1)}) %tuple.132, (f32[10,384,384]{2,1,0:T(8,128)}, ...), branch_computations={%region_30.30_spmd, %region_31.33_spmd} | conditional | flops 2719383552 | bytes 9439856 | solution.py:277
  1111.5 13.1 %conditional.2 = (f32[384,384]{1,0:T(8,128)S(1)}, f32[384,384]{1,0:T(8,128)S(1)}, f32[384,384]{1,0:T(8,128)S(1)}, f32[384,384]{1,0:T(8,128)S(1)}) conditional(s32[]{:T(128)} %convert_element_type.301, (f32[384,384]{1,0:T(8,128)S(1)}, f32[384,384]{1,0:T(8,128)S(1)}, f32[384,384]{1,0:T(8,128)S(1)}) %tuple.132, (f32[10,384,384]{2,1,0:T(8,128)}, ...), branch_computations={%region_30.30_spmd, %region_31.33_spmd} | conditional | flops 2719383552 | bytes 9439856 | solution.py:277
  1131.6 13.1 %conditional.2 = (f32[384,384]{1,0:T(8,128)S(1)}, f32[384,384]{1,0:T(8,128)S(1)}, f32[384,384]{1,0:T(8,128)S(1)}, f32[384,384]{1,0:T(8,128)S(1)}) conditional(s32[]{:T(128)} %convert_element_type.301, (f32[384,384]{1,0:T(8,128)S(1)}, f32[384,384]{1,0:T(8,128)S(1)}, f32[384,384]{1,0:T(8,128)S(1)}) %tuple.132, (f32[10,384,384]{2,1,0:T(8,128)}, ...), branch_computations={%region_30.30_spmd, %region_31.33_spmd} | conditional | flops 2719383552 | bytes 9439856 | solution.py:277
  1151.6 13.1 %conditional.2 = (f32[384,384]{1,0:T(8,128)S(1)}, f32[384,384]{1,0:T(8,128)S(1)}, f32[384,384]{1,0:T(8,128)S(1)}, f32[384,384]{1,0:T(8,128)S(1)}) conditional(s32[]{:T(128)} %convert_element_type.301, (f32[384,384]{1,0:T(8,128)S(1)}, f32[384,384]{1,0:T(8,128)S(1)}, f32[384,384]{1,0:T(8,128)S(1)}) %tuple.132, (f32[10,384,384]{2,1,0:T(8,128)}, ...), branch_computations={%region_30.30_spmd, %region_31.33_spmd} | conditional | flops 2719383552 | bytes 9439856 | solution.py:277
  (382 shorter events, 542.6 us)
Async XLA Ops:
  7.2 83.7 %all-gather.2.cloned.1.call-start = ((), (), s32[]{:S(2)}) async-start(), calls=%async_computation.1 | async-start | bytes 8847360 | tf_op jit(solution)/shard_map/all_gather | solution.py:147
  12.1 838.4 %all-reduce.2.cloned.1.call-start = ((), (), s32[]{:S(2)}) async-start(), calls=%async_computation.2 | async-start | bytes 21233664 | tf_op jit(solution)/shard_map/psum | solution.py:248
  15.0 105.8 %copy-start.29 = (f32[2,1024]{1,0:T(2,128)}, f32[2,1024]{1,0:T(2,128)S(1)}, u32[]{:S(2)}) copy-start(f32[2,1024]{1,0:T(2,128)S(1)} %broadcast_multiply_fusion.6) | copy-start | bytes 24580
  16.0 104.9 %copy-start.32 = (f32[2,1024]{1,0:T(2,128)}, f32[2,1024]{1,0:T(2,128)S(1)}, u32[]{:S(2)}) copy-start(f32[2,1024]{1,0:T(2,128)S(1)} %add_rsqrt_fusion.1) | copy-start | bytes 24580
  110.8 10.9 copy-start.9
  110.9 12.1 slice-start.2
  112.1 16.3 %copy-start.34 = (f32[2,384]{1,0:T(2,128)}, f32[2,384]{1,0:T(2,128)S(1)}, u32[]{:S(2)}) copy-start(f32[2,384]{1,0:T(2,128)S(1)} %get-tuple-element.418) | copy-start | bytes 9220
  205.9 17.1 %copy-start.21 = (bf16[2,1024,384]{2,1,0:T(8,128)(2,1)}, bf16[2,1024,384]{2,1,0:T(8,128)(2,1)S(1)}, u32[]{:S(2)}) copy-start(bf16[2,1024,384]{2,1,0:T(8,128)(2,1)S(1)} %add_convert_fusion.3) | copy-start | bytes 4718596
  223.0 12.7 %copy-start.19 = (bf16[4,384,384]{2,1,0:T(8,128)(2,1)S(1)}, bf16[4,384,384]{2,1,0:T(8,128)(2,1)}, u32[]{:S(2)}) copy-start(bf16[4,384,384]{2,1,0:T(8,128)(2,1)} %get-tuple-element.404) | copy-start | bytes 3538948
  223.0 12.7 %copy-start.52 = (f32[384]{0:T(512)S(1)}, f32[384]{0:T(512)}, u32[]{:S(2)}) copy-start(f32[384]{0:T(512)} %get-tuple-element.412) | copy-start | bytes 4612
  235.7 9.8 copy-start.22
  290.0 12.0 copy-start.1
  448.1 12.0 copy-start.1
  602.9 9.6 copy-start.8
  602.9 9.6 copy-start.26
  602.9 9.6 copy-start.30
  602.9 9.6 copy-start.33
  602.9 9.6 copy-start.35
  647.8 378.4 %reduce-scatter.2.cloned.1.call-start = ((), (), s32[]{:S(2)}) async-start(), calls=%async_computation.3 | async-start | bytes 17694720 | tf_op jit(solution)/shard_map/reduce_scatter | solution.py:249
  888.4 44.6 %copy-start.28 = (f32[5760]{0:T(1024)S(1)}, f32[5760]{0:T(1024)}, u32[]{:S(2)}) copy-start(f32[5760]{0:T(1024)} %param.29) | copy-start | bytes 69124
  888.4 44.6 %copy-start.39 = (f32[5760]{0:T(1024)S(1)}, f32[5760]{0:T(1024)}, u32[]{:S(2)}) copy-start(f32[5760]{0:T(1024)} %param.31) | copy-start | bytes 69124
  888.5 44.5 %copy-start.40 = (f32[5760]{0:T(1024)S(1)}, f32[5760]{0:T(1024)}, u32[]{:S(2)}) copy-start(f32[5760]{0:T(1024)} %param.30) | copy-start | bytes 69124
  888.5 45.2 %copy-start.10 = (bf16[384,6,384]{0,2,1:T(8,128)(2,1)S(1)}, bf16[384,6,384]{0,2,1:T(8,128)(2,1)}, u32[]{:S(2)}) copy-start(bf16[384,6,384]{0,2,1:T(8,128)(2,1)} %copy-done.9) | copy-start | bytes 5308420
  933.0 93.2 %copy-start.31 = (f32[5760]{0:T(1024)}, f32[5760]{0:T(1024)S(1)}, u32[]{:S(2)}) copy-start(f32[5760]{0:T(1024)S(1)} %psum.15) | copy-start | bytes 69124
  (40 other events, 171.3 us)
Sparse Core Ops, SparseCore 0:
  12.2 78.6 all-gather.1
  647.9 202.5 all-reduce.1
  888.6 137.4 reduce-scatter.1
where the time goes:
time: 1250 us; the launch traced here: 1230 us
  matrix products  513 us (41%)
  waiting for transfers between devices  369 us (30%)
  local copies, waits for them, and re-layouts  188 us (15%)
  other arithmetic  81.5 us (7%)
  blocking collectives  41.1 us (3%)
  loops' own time  26.6 us (2%)
  between operations  14.9 us (1%)
    psum x1, waiting for transfers between devices, per_device(): summed = lax.psum(block_grads, 'dp')  203 us
    dot_general x4, matrix products, attend_back(): jnp.einsum('hqk,khd->qhd', back_scores, keys, preferred_element_type=jnp....  133 us
    dot_general x4, matrix products, attend_back(): jnp.einsum('hqk,qhd->khd', back_scores, block_rows, preferred_element_typ...  109 us
    reduce_scatter x1, waiting for transfers between devices, per_device(): lax.psum_scatter(jnp.zeros((total_slots, D, D), jnp.float32).at[places].s...  91.6 us
    all_gather x1, waiting for transfers between devices, per_device(): lax.all_gather(master.astype(jnp.bfloat16), 'own', axis=0, tiled=True)  74.9 us
    psum x1, blocking collectives, per_device(): bias_grad = lax.psum(bias_grads, ('dp', 'own'))  41.1 us
    dot_general x5, matrix products, product(): return jnp.dot(left_side, right_side, preferred_element_type=jnp.float32)  35.9 us
    squeeze x30, local copies, waits for them, and re-layouts, per_device(): lax.map(renew, (jnp.arange(slot_count, dtype=jnp.int32), owned_grads, sta...  33.3 us
  transfers between devices with their start and end apart: 3, of which 3 were waited for; matrix products, arithmetic and copies ran while one was open for 1% of the time, Pallas kernels for 0%

commit v1 on v0

v1 whole, which is shorter than its diff:
```python
import functools

import jax
import jax.numpy as jnp
from jax import lax
from jax.experimental import pallas as pl
from jax.experimental.pallas import tpu as pltpu
from jax.sharding import PartitionSpec as P

D = 384
H = 6
HD = 64
FF = 1536
FB = FF // D
STEP = 10
HALF = D // 2
LATE = 4
EARLY = 2 * FB

norm_eps = 1e-06
shampoo_rate = 1.0
shampoo_decay = 0.01
adam_rate = 0.2
adam_decay = 0.01
f32 = jnp.float32
bf16 = jnp.bfloat16
VMEM = 56 * 1024 * 1024

NN = (((1,), (0,)), ((), ()))
NT = (((1,), (1,)), ((), ()))
TN = (((0,), (0,)), ((), ()))


def dot(left, right, dims=NN):
    return lax.dot_general(left, right, dims, preferred_element_type=f32)


def cost(flops, moved, trans=0):
    return pl.CostEstimate(flops=int(flops), bytes_accessed=int(moved), transcendentals=int(trans))


def params(**more):
    return pltpu.CompilerParams(vmem_limit_bytes=VMEM, **more)


def shape(dims, dtype=f32):
    return jax.ShapeDtypeStruct(dims, dtype)


class Net:
    def __init__(self, n_dp, n_own):
        self.n_dp, self.n_own = n_dp, n_own
        self.dp_bits = [1 << i for i in range(n_dp.bit_length() - 1)]
        self.own_bits = [1 << i for i in range(n_own.bit_length() - 1)]
        core = [("dp", self.dp_bits[0])]
        plane = [("dp", self.dp_bits[1]), ("own", self.own_bits[0])]
        line = [("dp", self.dp_bits[2]), ("dp", self.dp_bits[3])]
        self.stages = [core, plane, line]
        self.rest = [[("dp", b)] for b in self.dp_bits[4:]] + [
            [("own", b)] for b in self.own_bits[1:]
        ]

    def place(self, bits):
        at = {"dp": lax.axis_index("dp"), "own": lax.axis_index("own")}
        total = 0
        for i, (axis, bit) in enumerate(bits):
            total = total + jnp.where((at[axis] & bit) != 0, 1 << i, 0)
        return total.astype(jnp.int32)

    def swap(self, value, bits, which):
        dp_mask = own_mask = 0
        for i, (axis, bit) in enumerate(bits):
            if which >> i & 1:
                if axis == "dp":
                    dp_mask |= bit
                else:
                    own_mask |= bit
        pairs = []
        for d in range(self.n_dp):
            for o in range(self.n_own):
                source = d * self.n_own + o
                pairs.append((source, (d ^ dp_mask) * self.n_own + (o ^ own_mask)))
        return lax.ppermute(value, ("dp", "own"), pairs)

    def scatter_sum(self, parts, bits, link):
        me = self.place(bits)
        got = []
        for g in range(1 << len(bits)):
            piece = lax.dynamic_index_in_dim(parts, me ^ g, 0, keepdims=False)
            if g > 0:
                piece = self.swap(piece.astype(link), bits, g).astype(parts.dtype)
            got.append(piece)
        while len(got) > 1:
            got = [got[i] + got[i + 1] for i in range(0, len(got), 2)]
        return got[0]

    def gather(self, value, bits):
        return jnp.stack([value] + [self.swap(value, bits, g) for g in range(1, 1 << len(bits))])

    def add_up(self, value, bits):
        got = [value] + [self.swap(value, bits, g) for g in range(1, 1 << len(bits))]
        while len(got) > 1:
            got = [got[i] + got[i + 1] for i in range(0, len(got), 2)]
        return got[0]

    def own_list(self):
        return [("own", b) for b in self.own_bits]


def pick_kernel(table, master, out):
    kept = table[1, pl.program_id(0)] > 0

    @pl.when(kept)
    def _():
        out[...] = master[...].astype(bf16)

    @pl.when(jnp.logical_not(kept))
    def _():
        out[...] = jnp.zeros_like(out)


def pick_blocks(table, master, halves):
    count = table.shape[1]
    rows = HALF if halves else D
    return pl.pallas_call(
        pick_kernel,
        grid_spec=pltpu.PrefetchScalarGridSpec(
            num_scalar_prefetch=1,
            grid=(count,),
            in_specs=[
                pl.BlockSpec((1, rows, D), lambda i, t: (t[0, i], t[2, i] if halves else 0, 0))
            ],
            out_specs=pl.BlockSpec((1, rows, D), lambda i, t: (i, 0, 0)),
        ),
        out_shape=shape((count, rows, D), bf16),
        compiler_params=params(),
        cost_estimate=cost(0, count * rows * D * 6),
        name="pick_blocks",
    )(table, master)


def join_halves(core, near, far, out):
    out[:, pl.ds(pl.multiple_of(core * HALF, HALF), HALF), :] = near[...]
    out[:, pl.ds(pl.multiple_of((1 - core) * HALF, HALF), HALF), :] = far[...]


def normed(value):
    centered = value - jnp.mean(value, axis=-1, keepdims=True)
    inverse = lax.rsqrt(jnp.mean(centered * centered, axis=-1, keepdims=True) + norm_eps)
    return centered * inverse, inverse


def norm_back(gradient, norm, inverse):
    return inverse * (
        gradient
        - jnp.mean(gradient, axis=-1, keepdims=True)
        - norm * jnp.mean(gradient * norm, axis=-1, keepdims=True)
    )


def attend_kernel(core, latents, mod, near, far, bias, qkv, mixed, total, weight):
    @pl.when(pl.program_id(0) == 0)
    def _():
        join_halves(core[0], near, far, weight)

    norm, _ = normed(latents[0].astype(f32))
    first = (norm * (1.0 + mod[0, 1:2]) + mod[0, 0:1]).astype(bf16)
    for b in range(3):
        qkv[0, :, b * D : (b + 1) * D] = (dot(first, weight[b]) + bias[b : b + 1]).astype(bf16)
    lane = lax.broadcasted_iota(jnp.int32, (1, 2 * HD), 1)
    values_t = qkv[0, :, 2 * D : 3 * D].T
    total[0] = jnp.zeros_like(total[0])
    for p in range(H // 2):
        keys = qkv[0, :, D + 2 * HD * p : D + 2 * HD * (p + 1)]
        pair = qkv[0, :, 2 * HD * p : 2 * HD * (p + 1)]
        for h in range(2):
            j = 2 * p + h
            mask = jnp.where((lane < HD) == (h == 0), HD**-0.5, 0.0).astype(bf16)
            scores = dot(keys, pair * mask, NT)
            peak = jnp.max(scores, axis=0, keepdims=True)
            expo = jnp.exp(scores - peak)
            sums = jnp.sum(expo, axis=0, keepdims=True)
            out = dot(values_t[HD * j : HD * (j + 1)], expo.astype(bf16))
            mixed[0, HD * j : HD * (j + 1), :] = (out * (1.0 / sums)).astype(bf16)
            total[0, j : j + 1, :] = peak + jnp.log(sums)


def middle_kernel(
    rows,
    core,
    latents,
    upstream,
    mixed,
    mod,
    near,
    far,
    bias,
    block_out,
    residual_back,
    mixed_back,
    delta,
    sums,
    grad_early,
    grad_proj,
    bias_sums,
    weight,
    second_s,
    act_s,
    pre_s,
    attn_s,
    ffn_s,
):
    step = pl.program_id(0)

    @pl.when(step == 0)
    def _():
        join_halves(core[0], near, far, weight)

    gate_one, shift_two, scale_two, gate_two = (mod[0, i : i + 1] for i in (2, 3, 4, 5))
    length = latents.shape[1]
    back_gate_two = back_gate_one = back_scale = back_shift = 0.0
    low_ffn = low_attn = 0.0
    low_pre = [0.0] * FB

    def column(value):
        return jnp.sum(value, axis=0, keepdims=True)

    for start in range(0, length, rows):
        part = slice(start, start + rows)
        attn_out = dot(mixed[0, :, part], weight[0], TN) + bias[3:4]
        residual = latents[0, part].astype(f32) + gate_one * attn_out
        norm, inverse = normed(residual)
        second = (norm * (1.0 + scale_two) + shift_two).astype(bf16)
        second_s[part] = second
        ct = upstream[0, part].astype(f32)
        ffn_back = (ct * gate_two).astype(bf16)
        ffn_s[part] = ffn_back
        ffn_out = bias[8:9]
        second_back = 0.0
        for n in range(FB):
            cols = slice(n * D, (n + 1) * D)
            pre = dot(second, weight[1 + n]) + bias[4 + n : 5 + n]
            square = pre * pre
            k0 = 0.7978845608028654
            tanh = jnp.tanh(pre * (k0 + (k0 * 0.044715) * square))
            half = 0.5 + 0.5 * tanh
            act = (pre * half).astype(bf16)
            slope = half + pre * (0.5 - 0.5 * tanh * tanh) * (
                k0 + (3.0 * k0 * 0.044715) * square
            )
            act_s[part, cols] = act
            ffn_out = ffn_out + dot(act, weight[1 + FB + n])
            act_back = dot(ffn_back, weight[1 + FB + n], NT)
            pre_back_f = act_back * slope
            pre_back = pre_back_f.astype(bf16)
            pre_s[part, cols] = pre_back
            low_pre[n] = low_pre[n] + column(pre_back.astype(f32))
            second_back = second_back + dot(pre_back, weight[1 + n], NT)
        block_out[0, part] = (residual + gate_two * ffn_out).astype(bf16)
        back_gate_two = back_gate_two + column(ct * ffn_out)
        back_scale = back_scale + column(second_back * norm)
        back_shift = back_shift + column(second_back)
        res_back = ct + norm_back(second_back * (1.0 + scale_two), norm, inverse)
        residual_back[0, part] = res_back
        back_gate_one = back_gate_one + column(res_back * attn_out)
        attn_back = (res_back * gate_one).astype(bf16)
        attn_s[part] = attn_back
        low_ffn = low_ffn + column(ffn_back.astype(f32))
        low_attn = low_attn + column(attn_back.astype(f32))
        mix_back = dot(attn_back, weight[0], NT).astype(bf16)
        mixed_back[0, part] = mix_back
        turned = mix_back.astype(f32).T * mixed[0, :, part].astype(f32)
        for j in range(H):
            delta[0, j : j + 1, part] = jnp.sum(
                turned[HD * j : HD * (j + 1)], axis=0, keepdims=True
            )
        delta[0, H:8, part] = jnp.zeros((8 - H, rows), f32)

    sums[0] = jnp.concatenate(
        [back_gate_one, back_shift, back_scale, back_gate_two, jnp.zeros((4, D), f32)], axis=0
    )
    biases = jnp.concatenate(
        [low_attn] + low_pre + [low_ffn, jnp.zeros((8 - FB - 2, D), f32)], axis=0
    )

    def store(first):
        def put(ref, index, value):
            ref[index] = value if first else ref[index] + value

        put(bias_sums, Ellipsis, biases)
        put(grad_proj, 0, dot(mixed[0], attn_s[...]))
        for n in range(FB):
            cols = slice(n * D, (n + 1) * D)
            put(grad_early, n, dot(second_s[...], pre_s[:, cols], TN))
            put(grad_early, FB + n, dot(act_s[:, cols], ffn_s[...], TN))

    @pl.when(step == 0)
    def _():
        store(True)

    @pl.when(step > 0)
    def _():
        store(False)


def attend_back_kernel(query, keys, values, back, total, delta, *rest):
    back_query, back_keys, back_values = rest[-3:]
    pair = rest[0]
    lane = lax.broadcasted_iota(jnp.int32, (1, 2 * HD), 1)
    keys_t = keys[0].T
    key_sum = value_sum = 0.0
    query_parts = []
    row = lax.broadcasted_iota(jnp.int32, (8, 1), 0)
    for h in range(2):
        one = jnp.where((lane < HD) == (h == 0), 1.0, 0.0).astype(bf16)
        pick = row == 2 * pair + h
        log_total = jnp.sum(jnp.where(pick, total[0], 0.0), axis=0, keepdims=True)
        row_delta = jnp.sum(jnp.where(pick, delta[0], 0.0), axis=0, keepdims=True)
        q = query[0] * (one * HD**-0.5)
        g = back[0] * one
        scores = dot(keys[0], q, NT)
        prob = jnp.exp(scores - log_total)
        prob_back = dot(values[0], g, NT)
        score_back = (prob * (prob_back - row_delta)).astype(bf16)
        value_sum = value_sum + dot(prob.astype(bf16), g)
        key_sum = key_sum + dot(score_back, q)
        query_parts.append(dot(keys_t[HD * h : HD * (h + 1)], score_back))
    back_keys[0] = key_sum.astype(bf16)
    back_values[0] = value_sum.astype(bf16)
    back_query[0] = (jnp.concatenate(query_parts, axis=0) * HD**-0.5).T.astype(bf16)


def first_back_kernel(
    core,
    latents,
    residual_back,
    mod,
    back_query,
    back_keys,
    back_values,
    near,
    far,
    grad_proj,
    latents_grad,
    sums,
    grads,
    bias_sums,
    weight,
):
    step = pl.program_id(0)

    @pl.when(step == 0)
    def _():
        join_halves(core[0], near, far, weight)
        grads[3] = grad_proj[0]

    norm, inverse = normed(latents[0].astype(f32))
    first = (norm * (1.0 + mod[0, 1:2]) + mod[0, 0:1]).astype(bf16)
    backs = (back_query[0], back_keys[0], back_values[0])
    new = [dot(first, b, TN) for b in backs]
    lows = jnp.concatenate(
        [jnp.sum(b.astype(f32), axis=0, keepdims=True) for b in backs]
        + [jnp.zeros((5, D), f32)],
        axis=0,
    )

    @pl.when(step == 0)
    def _():
        for i in range(3):
            grads[i] = new[i]
        bias_sums[...] = lows

    @pl.when(step > 0)
    def _():
        for i in range(3):
            grads[i] += new[i]
        bias_sums[...] += lows

    first_back = sum(dot(b, weight[i], NT) for i, b in enumerate(backs))
    sums[0] = jnp.concatenate(
        [
            jnp.sum(first_back, axis=0, keepdims=True),
            jnp.sum(first_back * norm, axis=0, keepdims=True),
            jnp.zeros((6, D), f32),
        ],
        axis=0,
    )
    latents_grad[0] = residual_back[0] + norm_back(
        first_back * (1.0 + mod[0, 1:2]), norm, inverse
    )


def split_two(value):
    high = value.astype(bf16)
    return high, (value - high.astype(f32)).astype(bf16)


def renew(gradient, state, outs):
    left, right, root_left, root_right, master = state
    grads_out, left_out, right_out, master_out = outs
    low = gradient.astype(bf16)
    grads_out[0] = gradient
    left_out[0] = 0.5 * left[0] + 0.5 * dot(low, low, NT)
    right_out[0] = 0.5 * right[0] + 0.5 * dot(low, low, TN)
    left_high, left_low = split_two(root_left[0])
    right_high, right_low = split_two(root_right[0])
    inner = dot(left_high, low) + dot(left_low, low)
    inner_high, inner_low = split_two(inner)
    direction = dot(inner_high, right_high) + dot(inner_low, right_high) + dot(inner_high, right_low)
    weight = master[0]
    scale = jnp.sqrt(jnp.mean(weight * weight) + norm_eps) * lax.rsqrt(
        jnp.mean(direction * direction) + norm_eps
    )
    master_out[0] = weight - shampoo_rate * (scale * direction + shampoo_decay * weight)


def keep_slot(table, given, outs):
    @pl.when((table[1, 0] == 0) & (pl.program_id(0) == 0))
    def _():
        for before, out in zip(given, outs):
            pltpu.sync_copy(before.at[pl.ds(table[0, 0], 1)], out)


def summed_slots_kernel(pieces, table, *refs):
    parts, state, outs = refs[:pieces], refs[pieces : pieces + 5], refs[-4:]
    keep_slot(table, refs[pieces + 5 : -4], outs)

    @pl.when(table[1, pl.program_id(0)] > 0)
    def _():
        gradient = jnp.concatenate([p[0, 0, 0] for p in parts], axis=0).astype(f32)
        renew(gradient, state, outs)


def cond_slots_kernel(table, cond, mods, *refs):
    state, outs = refs[:5], refs[-4:]
    keep_slot(table, refs[5:-4], outs)
    kind = table[1, pl.program_id(0)]

    @pl.when(kind == 1)
    def _():
        renew(dot(cond[...], mods[...], TN), state, outs)

    @pl.when(kind == 2)
    def _():
        left, right, _, _, master = state
        outs[0][0] = jnp.zeros_like(outs[0][0])
        outs[1][0] = 0.5 * left[0]
        outs[2][0] = 0.5 * right[0]
        outs[3][0] = master[0] - shampoo_rate * (shampoo_decay * master[0])


def slot_call(kernel, table, lead, lead_specs, state, outs, name):
    slots = state[0].shape[0]
    slot_spec = pl.BlockSpec((1, D, D), lambda i, t: (t[0, i], 0, 0))
    given = [] if outs is None else list(outs)
    steps = table.shape[1]
    first = 1 + len(lead) + 5
    return pl.pallas_call(
        kernel,
        grid_spec=pltpu.PrefetchScalarGridSpec(
            num_scalar_prefetch=1,
            grid=(steps,),
            in_specs=lead_specs
            + [slot_spec] * 5
            + [pl.BlockSpec(memory_space=pl.ANY)] * len(given),
            out_specs=[slot_spec] * 4,
        ),
        out_shape=[shape((slots, D, D))] * 4,
        input_output_aliases={first + i: i for i in range(len(given))},
        compiler_params=params(),
        cost_estimate=cost(steps * 7 * 2 * D**3, steps * 10 * D * D * 4),
        name=name,
    )(table, *lead, *state, *given)


def slot_places(owner, slot_count):
    order = jnp.arange(owner.shape[0], dtype=jnp.int32)
    before = (order[None, :] < order[:, None]) & (owner[None, :] == owner[:, None])
    return owner * slot_count + jnp.sum(before.astype(jnp.int32), axis=1)


def slot_table(blocks, mine, local, kinds, steps):
    work = kinds > 0
    rank = jnp.cumsum(work.astype(jnp.int32)) - 1
    count = rank[-1] + 1
    step = jnp.minimum(jnp.arange(steps, dtype=jnp.int32), jnp.maximum(count - 1, 0))
    hit = (rank[None, :] == step[:, None]) & work[None, :]
    live = (jnp.arange(steps, dtype=jnp.int32) < count).astype(jnp.int32)

    def choose(values):
        return jnp.sum(jnp.where(hit, values[None, :], 0), axis=1).astype(jnp.int32)

    return jnp.stack([choose(local), choose(kinds) * live, choose(blocks)])


def per_device(
    net,
    latents,
    condition,
    cotangent,
    owner,
    master,
    stat_left,
    stat_right,
    root_left,
    root_right,
    bias,
    moment_one,
    moment_two,
):
    slots = master.shape[0]
    seqs, length, _ = latents.shape
    tokens = seqs * length
    blocks = owner.shape[0]
    ada = blocks - 4 - EARLY
    member = lax.axis_index("own").astype(jnp.int32)
    core = net.place(net.stages[0])
    places = slot_places(owner, slots)
    mine = owner == member
    local = jnp.where(mine, places - member * slots, 0).astype(jnp.int32)
    table = jnp.stack(
        [local, mine.astype(jnp.int32), jnp.broadcast_to(core, (blocks,)).astype(jnp.int32)]
    )
    core_one = core.reshape(1)
    own_all = net.own_list()

    near_qkv = pick_blocks(table[:, 0:3], master, True)
    own_ada = pick_blocks(table[:, 4 + EARLY :], master, False)
    near_rest = pick_blocks(table[:, 3 : 4 + EARLY], master, True)
    for bit in own_all:
        near_qkv = near_qkv + net.swap(near_qkv, [bit], 1)
    far_qkv = net.swap(near_qkv, net.stages[0], 1)

    bias_rows = bias.reshape(-1, D)
    cond_float = condition.astype(f32)
    silu_cond, silu_pull = jax.vjp(jax.nn.silu, cond_float)
    cond_low = silu_cond.astype(bf16)
    cond_group = net.gather(cond_low, own_all)
    mod_parts = jnp.einsum("gld,bde->glbe", cond_group, own_ada, preferred_element_type=f32)
    modulation = mod_parts[0]
    for g in range(1, net.n_own):
        modulation = modulation + net.swap(mod_parts[g], own_all, g)
    modulation = modulation + bias_rows[9:]

    for bit in own_all:
        near_rest = near_rest + net.swap(near_rest, [bit], 1)
    far_rest = net.swap(near_rest, net.stages[0], 1)

    def whole(*dims):
        return pl.BlockSpec(dims, lambda i, *_: (0,) * len(dims))

    def each(*dims):
        return pl.BlockSpec((1,) + dims, lambda i, *_: (i,) + (0,) * len(dims))

    smem = pl.BlockSpec(memory_space=pltpu.SMEM)
    tok = each(length, D)
    qkv, mixed, totals = pl.pallas_call(
        attend_kernel,
        grid=(seqs,),
        in_specs=[
            smem,
            tok,
            each(6, D),
            whole(3, HALF, D),
            whole(3, HALF, D),
            whole(*bias_rows.shape),
        ],
        out_specs=[each(length, 3 * D), each(D, length), each(8, length)],
        out_shape=[
            shape((seqs, length, 3 * D), bf16),
            shape((seqs, D, length), bf16),
            shape((seqs, 8, length)),
        ],
        scratch_shapes=[pltpu.VMEM((3, D, D), bf16)],
        compiler_params=params(),
        cost_estimate=cost(16e9, 12e6, 12e6),
        name="attend",
    )(core_one, latents, modulation, near_qkv, far_qkv, bias_rows)

    (
        block_out,
        residual_back,
        mixed_back,
        delta,
        mid_sums,
        grad_early,
        grad_proj,
        mid_bias,
    ) = pl.pallas_call(
        functools.partial(middle_kernel, 256),
        grid=(seqs,),
        in_specs=[
            smem,
            tok,
            tok,
            each(D, length),
            each(6, D),
            whole(1 + EARLY, HALF, D),
            whole(1 + EARLY, HALF, D),
            whole(*bias_rows.shape),
        ],
        out_specs=[
            tok,
            tok,
            tok,
            each(8, length),
            each(8, D),
            whole(EARLY, D, D),
            whole(1, D, D),
            whole(8, D),
        ],
        out_shape=[
            shape((seqs, length, D), bf16),
            shape((seqs, length, D)),
            shape((seqs, length, D), bf16),
            shape((seqs, 8, length)),
            shape((seqs, 8, D)),
            shape((EARLY, D, D)),
            shape((1, D, D)),
            shape((8, D)),
        ],
        scratch_shapes=[
            pltpu.VMEM((1 + EARLY, D, D), bf16),
            pltpu.VMEM((length, D), bf16),
            pltpu.VMEM((length, FF), bf16),
            pltpu.VMEM((length, FF), bf16),
            pltpu.VMEM((length, D), bf16),
            pltpu.VMEM((length, D), bf16),
        ],
        compiler_params=params(),
        cost_estimate=cost(22e9, 25e6, 3e6),
        name="middle",
    )(core_one, latents, cotangent, mixed, modulation, near_rest, far_rest, bias_rows)

    def reduce_scatter(grads):
        rows = grads.shape[0] * D
        value = grads.reshape(2, rows // 2, D)
        value = net.scatter_sum(value, net.stages[0], f32)
        value = net.scatter_sum(value.reshape(4, rows // 8, D), net.stages[1], bf16)
        value = net.scatter_sum(value.reshape(4, rows // 32, D), net.stages[2], f32)
        for bits in net.rest:
            value = net.add_up(value, bits)
        return value.astype(bf16)

    def all_gather(value):
        for bits in net.stages[::-1]:
            value = net.gather(value, bits)
        return value

    early = all_gather(reduce_scatter(grad_early))

    backs = None
    for s in range(seqs):
        for p in range(H // 2):
            def head(offset, s=s, p=p):
                return pl.BlockSpec((1, length, 2 * HD), lambda i: (s, 0, offset + p))

            stat = pl.BlockSpec((1, 8, length), lambda i, s=s: (s, 0, 0))
            given = [] if backs is None else list(backs)

            def kernel(*refs, p=p):
                attend_back_kernel(*refs[:6], p, *refs[6:])

            backs = pl.pallas_call(
                kernel,
                grid=(1,),
                in_specs=[head(0), head(3), head(6), head(0), stat, stat]
                + [pl.BlockSpec(memory_space=pl.ANY)] * len(given),
                out_specs=[head(0)] * 3,
                out_shape=[shape((seqs, length, D), bf16)] * 3,
                input_output_aliases={6 + i: i for i in range(len(given))},
                compiler_params=params(),
                cost_estimate=cost(5e9, 2e6, 2e6),
                name="attend_back",
            )(qkv, qkv, qkv, mixed_back, totals, delta, *given)

    latents_grad, first_sums, grad_late, first_bias = pl.pallas_call(
        first_back_kernel,
        grid=(seqs,),
        in_specs=[
            smem,
            tok,
            tok,
            each(6, D),
            tok,
            tok,
            tok,
            whole(3, HALF, D),
            whole(3, HALF, D),
            whole(1, D, D),
        ],
        out_specs=[tok, each(8, D), whole(LATE, D, D), whole(8, D)],
        out_shape=[
            shape((seqs, length, D)),
            shape((seqs, 8, D)),
            shape((LATE, D, D)),
            shape((8, D)),
        ],
        scratch_shapes=[pltpu.VMEM((3, D, D), bf16)],
        compiler_params=params(),
        cost_estimate=cost(5e9, 18e6),
        name="first_back",
    )(core_one, latents, residual_back, modulation, *backs, near_qkv, far_qkv, grad_proj)

    late = all_gather(reduce_scatter(grad_late))

    back_mod = jnp.concatenate(
        [first_sums[:, 0:2].reshape(seqs, 2 * D), mid_sums[:, 0:4].reshape(seqs, 4 * D)], axis=1
    ).astype(bf16)
    rows = jnp.concatenate([back_mod, cond_low], axis=1)
    every = net.stages + net.rest
    for bits in every[::-1]:
        rows = net.gather(rows, bits)
    order = []
    for bits in every:
        order = order + bits[::-1]
    digits = len(order)
    group_rows = []
    flat = rows.reshape(1 << digits, seqs, (ada + 1) * D)
    for g in range(net.n_own):
        at = 0
        for k, (axis, bit) in enumerate(order):
            if axis == "own" and g & bit:
                at |= 1 << (digits - 1 - k)
        group_rows.append(flat[at])
    me = net.place(order[::-1])
    devices = 1 << digits
    number = jnp.arange(devices * seqs, dtype=jnp.int32)
    turn = (
        (number[:, None] // seqs ^ me) == number[None, :] // seqs
    ) & (number[:, None] % seqs == number[None, :] % seqs)
    sorted_rows = dot(
        turn.astype(bf16), rows.reshape(devices * seqs, (ada + 1) * D)
    ).astype(bf16)
    all_mods, all_cond = sorted_rows[:, : ada * D], sorted_rows[:, ada * D :]
    group = jnp.stack(group_rows)[:, :, : ada * D].reshape(net.n_own, seqs, ada, D)
    cond_parts = jnp.einsum("glbe,bde->gld", group, own_ada, preferred_element_type=f32)
    back_cond = cond_parts[0]
    for g in range(1, net.n_own):
        back_cond = back_cond + net.swap(cond_parts[g], own_all, g)
    condition_grad = silu_pull(back_cond)[0]

    bias_part = jnp.concatenate([first_bias[0:3], mid_bias[0 : FB + 2]], axis=0)
    for bits in every:
        bias_part = net.add_up(bias_part, bits)
    bias_grad = jnp.concatenate(
        [bias_part.reshape(-1), jnp.sum(all_mods.astype(f32), axis=0)]
    )

    state = (stat_left, stat_right, root_left, root_right, master)
    number = jnp.arange(blocks, dtype=jnp.int32)
    is_early = (number >= 4) & (number < 4 + EARLY)
    is_ada = number >= 4 + EARLY
    seat = [net.place(bits) for bits in net.stages]

    def gather_specs(value, count):
        per = 32 // count
        specs = []
        for i in range(per):
            def where(s, t, i=i):
                shard = t[2, s] * per + i
                return (
                    (shard // 16) ^ t[3, 0],
                    (shard // 4 % 4) ^ t[3, 1],
                    (shard % 4) ^ t[3, 2],
                    0,
                    0,
                )

            specs.append(pl.BlockSpec((1, 1, 1) + value.shape[3:], where))
        return [value] * per, specs

    def with_seat(given):
        row = jnp.zeros((1, given.shape[1]), jnp.int32)
        for i in range(3):
            row = row.at[0, i].set(seat[i])
        return jnp.concatenate([given, row], axis=0)

    def steps_of(count):
        return max(3, min(slots, count))

    early_table = with_seat(
        slot_table(number - 4, mine, local, (mine & is_early).astype(jnp.int32), steps_of(EARLY))
    )
    lead, specs = gather_specs(early, EARLY)
    outs = slot_call(
        functools.partial(summed_slots_kernel, len(lead)),
        early_table,
        lead,
        specs,
        state,
        None,
        "early_slots",
    )

    filled = jnp.sum(mine.astype(jnp.int32))
    empty = jnp.arange(slots, dtype=jnp.int32)
    cond_table = slot_table(
        jnp.concatenate([jnp.maximum(number - 4 - EARLY, 0), jnp.zeros_like(empty)]),
        None,
        jnp.concatenate([local, empty]),
        jnp.concatenate(
            [(mine & is_ada).astype(jnp.int32), jnp.where(empty >= filled, 2, 0)]
        ).astype(jnp.int32),
        slots,
    )
    count_rows = devices * seqs
    outs = slot_call(
        cond_slots_kernel,
        cond_table,
        [all_cond, all_mods],
        [
            pl.BlockSpec((count_rows, D), lambda i, t: (0, 0)),
            pl.BlockSpec((count_rows, D), lambda i, t: (0, t[2, i])),
        ],
        state,
        outs,
        "cond_slots",
    )

    late_table = with_seat(
        slot_table(number, mine, local, (mine & (number < 4)).astype(jnp.int32), steps_of(LATE))
    )
    lead, specs = gather_specs(late, LATE)
    weight_grads, left_new, right_new, master_new = slot_call(
        functools.partial(summed_slots_kernel, len(lead)),
        late_table,
        lead,
        specs,
        state,
        outs,
        "late_slots",
    )

    moment_one_new = 0.9 * moment_one + 0.1 * bias_grad
    moment_two_new = 0.95 * moment_two + 0.05 * bias_grad * bias_grad
    corrected = (
        moment_one_new / (1.0 - 0.9**STEP) / (jnp.sqrt(moment_two_new / (1.0 - 0.95**STEP)) + 1e-08)
    )
    bias_new = bias - adam_rate * (corrected + adam_decay * bias)
    return (
        block_out,
        latents_grad,
        condition_grad,
        weight_grads,
        left_new,
        right_new,
        master_new,
        bias_grad,
        moment_one_new,
        moment_two_new,
        bias_new,
    )


def solution(mesh):
    net = Net(mesh.shape["dp"], mesh.shape["own"])
    token = P(("dp", "own"), None, None)
    slot = P("own", None, None)
    return jax.shard_map(
        functools.partial(per_device, net),
        mesh=mesh,
        in_specs=(token, P(("dp", "own"), None), token, P()) + (slot,) * 5 + (P(),) * 3,
        out_specs=(token, token, P(("dp", "own"), None)) + (slot,) * 4 + (P(),) * 4,
        check_vma=False,
    )
```

time: 1250 us -> 345 us (0.28); the launches traced: 1230 us -> 343 us
  matrix products: 513 us -> 2.81 us
  waiting for transfers between devices: 369 us -> 36.6 us
  Pallas kernels: 0 us -> 182 us
  local copies, waits for them, and re-layouts: 188 us -> 21.1 us
  starting transfers between devices: 0.12 us -> 59.8 us
  other arithmetic: 81.5 us -> 33.1 us
  blocking collectives: 41.1 us -> 0 us
  loops' own time: 26.6 us -> 0 us
    dot_general x83 -> x3, matrix products: 513 us -> 2.81 us  [the longest x1 1.94 us: per_device(): jnp.einsum('gld,bde->glbe', cond_group, own_ada, preferred_element_type=f32)]
    psum x1 -> x0, waiting for transfers between devices: 203 us -> none  [per_device(): summed = lax.psum(block_grads, 'dp')]
    pallas_call x0 -> x15, Pallas kernels: none -> 182 us  [the longest x1 45.2 us: per_device(): pl.pallas_call(functools.partial(middle_kernel, 256), grid=(seqs,), in_sp...]
    reduce_scatter x1 -> x0, waiting for transfers between devices: 91.6 us -> none  [per_device(): lax.psum_scatter(jnp.zeros((total_slots, D, D), jnp.float32).at[places].s...]
    all_gather x1 -> x0, waiting for transfers between devices: 74.9 us -> none  [per_device(): lax.all_gather(master.astype(jnp.bfloat16), 'own', axis=0, tiled=True)]
    ppermute x0 -> x49, starting transfers between devices: none -> 59.8 us  [swap(): return lax.ppermute(value, ('dp', 'own'), pairs)]
    psum x1 -> x0, blocking collectives: 41.1 us -> none  [per_device(): bias_grad = lax.psum(bias_grads, ('dp', 'own'))]
    squeeze x33 -> x5, local copies, waits for them, and re-layouts: 39.7 us -> 2.75 us  [the longest x4 2.75 us: scatter_sum(): piece = lax.dynamic_index_in_dim(parts, me ^ g, 0, keepdims=False)]
  transfers between devices with their start and end apart: 3 -> 49, of which waited for: 3 -> 17; matrix products, arithmetic and copies ran while one was open for 1% -> 14% of each run, Pallas kernels for 0% -> 11%
where the time goes in v1:
time: 345 us; the launch traced here: 343 us
  Pallas kernels  182 us (53%)
  starting transfers between devices  59.8 us (17%)
  waiting for transfers between devices  36.6 us (11%)
  other arithmetic  33.1 us (10%)
  local copies, waits for them, and re-layouts  21.1 us (6%)
  between operations  6.75 us (2%)
    ppermute x49, starting transfers between devices, swap(): return lax.ppermute(value, ('dp', 'own'), pairs)  59.8 us
    pallas_call x1, Pallas kernels, per_device(): pl.pallas_call(functools.partial(middle_kernel, 256), grid=(seqs,), in_sp...  45.2 us
    pallas_call x6, Pallas kernels, per_device(): pl.pallas_call(kernel, grid=(1,), in_specs=[head(0), head(3), head(6), he...  44 us
    pallas_call x3, Pallas kernels, slot_call(): pl.pallas_call(kernel, grid_spec=pltpu.PrefetchScalarGridSpec(num_scalar_...  42.5 us
    ppermute x49, waiting for transfers between devices, swap(): return lax.ppermute(value, ('dp', 'own'), pairs)  36.6 us
    pallas_call x1, Pallas kernels, per_device(): pl.pallas_call(attend_kernel, grid=(seqs,), in_specs=[smem, tok, each(6,...  22.2 us
    pallas_call x3, Pallas kernels, pick_blocks(): pl.pallas_call(pick_kernel, grid_spec=pltpu.PrefetchScalarGridSpec(num_sc...  14.9 us
    pallas_call x1, Pallas kernels, per_device(): pl.pallas_call(first_back_kernel, grid=(seqs,), in_specs=[smem, tok, tok,...  13.6 us
  transfers between devices with their start and end apart: 49, of which 17 were waited for; matrix products, arithmetic and copies ran while one was open for 14% of the time, Pallas kernels for 11%

profile of v1, /device:TPU:0, one launch (start us, length us, event | category | flops | bytes accessed | tf_op | source)
XLA Modules:
  0.0 342.5 jit_solution(14674138219586536536)
XLA Ops:
  1.3 3.0 collective-permute-start
  8.0 3.2 pick_blocks.4
  12.3 6.0 %pick_blocks.5 = bf16[9,192,384]{2,1,0:T(8,128)(2,1)} custom-call(s32[3,9]{1,0:T(4,128)} %slice.183.table, f32[10,384,384]{2,1,0:T(8,128)} %refs_12_.1), custom_call_target="tpu_custom_call" | custom-call | bytes 3981312 | tf_op jit(solution)/shard_map/pick_blocks/pallas_call | solution.py:125
  50.6 5.7 %pick_blocks.3 = bf16[6,384,384]{2,1,0:T(8,128)(2,1)} custom-call(s32[3,6]{1,0:T(4,128)} %slice.177.table, f32[10,384,384]{2,1,0:T(8,128)} %refs_12_.1), custom_call_target="tpu_custom_call" | custom-call | bytes 5308416 | tf_op jit(solution)/shard_map/pick_blocks/pallas_call | solution.py:125
  65.5 22.2 %attend.1 = (bf16[2,1024,1152]{2,1,0:T(8,128)(2,1)}, bf16[2,384,1024]{2,1,0:T(8,128)(2,1)}, f32[2,8,1024]{2,1,0:T(8,128)}) custom-call(s32[1]{0:T(128)} %bitcast.core, bf16[2,1024,384]{2,1,0:T(8,128)(2,1)} %latents.5, f32[2,6,384]{2,1,0:T(8,128)} %fusion.24.mod, bf16[3,192,384]{2,1,0:T(8,128)(2,1)} %add.280.near, bf16[3,192,384]{2,1,0:T(8,128)(2,1)} %copy-done.16, ...), custom_call_target="tpu_custom_call" | custom-call | flops 16000000000 | bytes 12000000 | tf_op jit(solution)/shard_map/attend/pallas_call | solution.py:557
  88.8 45.2 %middle.1 = (bf16[2,1024,384]{2,1,0:T(8,128)(2,1)}, f32[2,1024,384]{2,1,0:T(8,128)}, bf16[2,1024,384]{2,1,0:T(8,128)(2,1)}, f32[2,8,1024]{2,1,0:T(8,128)}, f32[2...) custom-call(s32[1]{0:T(128)} %bitcast.core, ...), custom_call_target="tpu_custom_call" | custom-call | flops 22000001024 | bytes 25000000 | tf_op jit(solution)/shard_map/middle/pallas_call | solution.py:589
  134.8 7.3 %attend_back.6 = (bf16[2,1024,384]{2,1,0:T(8,128)(2,1)}, bf16[2,1024,384]{2,1,0:T(8,128)(2,1)}, bf16[2,1024,384]{2,1,0:T(8,128)(2,1)}) custom-call(bf16[2,1024,1152]{2,1,0:T(8,128)(2,1)} %get-tuple-element.131.refs_0_.refs_1_.refs_2_, bf16[2,1024,1152]{2,1,0:T(8,128)(2,1)} %get-tuple-element.131.refs_0_.refs_1_.refs_2_, ...), custom_call_target="tpu_custom_call" | custom-call | flops 5000000000 | bytes 2000000 | tf_op jit(solution)/shard_map/attend_back/pallas_call | solution.py:664
  142.1 7.3 %attend_back.7 = (bf16[2,1024,384]{2,1,0:T(8,128)(2,1)}, bf16[2,1024,384]{2,1,0:T(8,128)(2,1)}, bf16[2,1024,384]{2,1,0:T(8,128)(2,1)}) custom-call(bf16[2,1024,1152]{2,1,0:T(8,128)(2,1)} %get-tuple-element.131.refs_0_.refs_1_.refs_2_, ...), custom_call_target="tpu_custom_call", output_to_operand_aliasing={{0}: (6, {}), {1}: (7, {}), {2}: (8, {})} | custom-call | flops 5000000000 | bytes 2000000 | tf_op jit(solution)/shard_map/attend_back/pallas_call | solution.py:664
  149.3 7.6 %attend_back.8 = (bf16[2,1024,384]{2,1,0:T(8,128)(2,1)}, bf16[2,1024,384]{2,1,0:T(8,128)(2,1)}, bf16[2,1024,384]{2,1,0:T(8,128)(2,1)}) custom-call(bf16[2,1024,1152]{2,1,0:T(8,128)(2,1)} %get-tuple-element.131.refs_0_.refs_1_.refs_2_, ...), custom_call_target="tpu_custom_call", output_to_operand_aliasing={{0}: (6, {}), {1}: (7, {}), {2}: (8, {})} | custom-call | flops 5000000000 | bytes 2000000 | tf_op jit(solution)/shard_map/attend_back/pallas_call | solution.py:664
  157.0 7.3 %attend_back.9 = (bf16[2,1024,384]{2,1,0:T(8,128)(2,1)}, bf16[2,1024,384]{2,1,0:T(8,128)(2,1)}, bf16[2,1024,384]{2,1,0:T(8,128)(2,1)}) custom-call(bf16[2,1024,1152]{2,1,0:T(8,128)(2,1)} %get-tuple-element.131.refs_0_.refs_1_.refs_2_, ...), custom_call_target="tpu_custom_call", output_to_operand_aliasing={{0}: (6, {}), {1}: (7, {}), {2}: (8, {})} | custom-call | flops 5000000000 | bytes 2000000 | tf_op jit(solution)/shard_map/attend_back/pallas_call | solution.py:664
  164.2 7.2 %attend_back.10 = (bf16[2,1024,384]{2,1,0:T(8,128)(2,1)}, bf16[2,1024,384]{2,1,0:T(8,128)(2,1)}, bf16[2,1024,384]{2,1,0:T(8,128)(2,1)}) custom-call(bf16[2,1024,1152]{2,1,0:T(8,128)(2,1)} %get-tuple-element.131.refs_0_.refs_1_.refs_2_, ...), custom_call_target="tpu_custom_call", output_to_operand_aliasing={{0}: (6, {}), {1}: (7, {}), {2}: (8, {})} | custom-call | flops 5000000000 | bytes 2000000 | tf_op jit(solution)/shard_map/attend_back/pallas_call | solution.py:664
  171.4 7.4 %attend_back.11 = (bf16[2,1024,384]{2,1,0:T(8,128)(2,1)}, bf16[2,1024,384]{2,1,0:T(8,128)(2,1)}, bf16[2,1024,384]{2,1,0:T(8,128)(2,1)}) custom-call(bf16[2,1024,1152]{2,1,0:T(8,128)(2,1)} %get-tuple-element.131.refs_0_.refs_1_.refs_2_, ...), custom_call_target="tpu_custom_call", output_to_operand_aliasing={{0}: (6, {}), {1}: (7, {}), {2}: (8, {})} | custom-call | flops 5000000000 | bytes 2000000 | tf_op jit(solution)/shard_map/attend_back/pallas_call | solution.py:664
  178.8 13.6 %first_back.1 = (f32[2,1024,384]{2,1,0:T(8,128)}, f32[2,8,384]{2,1,0:T(8,128)}, f32[4,384,384]{2,1,0:T(8,128)}, f32[8,384]{1,0:T(8,128)}) custom-call(s32[1]{0:T(128)} %bitcast.core, bf16[2,1024,384]{2,1,0:T(8,128)(2,1)} %latents.5, f32[2,1024,384]{2,1,0:T(8,128)} %get-tuple-element.130.residual_back, f32[2,6,384]{2,1,0:T(8,128)} %fusion.24.mod, ...), custom_call_target="tpu_custom_call" | custom-call | flops 5000000000 | bytes 18000000 | tf_op jit(solution)/shard_map/first_back/pallas_call | solution.py:677
  210.7 3.7 %collective-permute-start.48 = (f32[9,384]{1,0:T(8,128)S(1)}, f32[9,384]{1,0:T(8,128)S(1)}, u32[]{:S(2)}, u32[]{:S(2)}) collective-permute-start(f32[9,384]{1,0:T(8,128)S(1)} %add_add_fusion.1), channel_id=1, source_target_pairs={{0,24},{1,25},{2,26},{3,27},{4,28},{5,29},{6,30},{7,31},{8,16},{9,... | collective-permute-start | bytes 41480 | tf_op jit(solution)/shard_map/ppermute | solution.py:83
  239.6 5.8 %collective-permute-done.31 = bf16[384,384]{1,0:T(8,128)(2,1)S(1)} collective-permute-done((bf16[384,384]{1,0:T(8,128)(2,1)S(1)}, bf16[384,384]{1,0:T(8,128)(2,1)S(1)}, u32[]{:S(2)}, u32[]{:S(2)}) %collective-permute-start.31) | collective-permute-done | bytes 294944 | tf_op jit(solution)/shard_map/ppermute | solution.py:83
  255.1 5.2 %collective-permute-start.18 = (f32[48,384]{1,0:T(8,128)S(1)}, f32[48,384]{1,0:T(8,128)S(1)}, u32[]{:S(2)}, u32[]{:S(2)}) collective-permute-start(f32[48,384]{1,0:T(8,128)S(1)} %get-tuple-element.210), channel_id=1, source_target_pairs={{0,8},{1,9},{2,10},{3,11},{4,12},{5,13},{6,14},{7,15},{8,0},{9,1},... | collective-permute-start | bytes 221192 | tf_op jit(solution)/shard_map/ppermute | solution.py:83
  260.3 5.2 %collective-permute-done.33 = f32[96,384]{1,0:T(8,128)S(1)} collective-permute-done((f32[96,384]{1,0:T(8,128)S(1)}, f32[96,384]{1,0:T(8,128)S(1)}, u32[]{:S(2)}, u32[]{:S(2)}) %collective-permute-start.33) | collective-permute-done | bytes 147488 | tf_op jit(solution)/shard_map/ppermute | solution.py:83
  265.5 3.0 collective-permute-start.37
  270.0 3.0 collective-permute-start.23
  282.4 3.3 collective-permute-done.39
  296.8 2.9 pad_maximum_fusion.refs_0_.refs_1_.refs_2_.refs_3_
  299.7 13.1 %early_slots.1 = (f32[10,384,384]{2,1,0:T(8,128)}, f32[10,384,384]{2,1,0:T(8,128)}, f32[10,384,384]{2,1,0:T(8,128)}, f32[10,384,384]{2,1,0:T(8,128)}) custom-call(s32[4,8]{1,0:T(4,128)} %pad_add_fusion.2.table, bf16[2,4,4,96,384]{4,3,2,1,0:T(8,128)(2,1)} %pad_maximum_fusion.refs_0_.refs_1_.refs_2_.refs_3_, ...), custom_call_target="tpu_custom_call" | custom-call | flops 6341787648 | bytes 47185920 | tf_op jit(solution)/shard_map/early_slots/pallas_call | solution.py:458
  312.8 20.8 %cond_slots.1 = (f32[10,384,384]{2,1,0:T(8,128)}, f32[10,384,384]{2,1,0:T(8,128)}, f32[10,384,384]{2,1,0:T(8,128)}, f32[10,384,384]{2,1,0:T(8,128)}) custom-call(s32[3,10]{1,0:T(4,128)} %pad_add_fusion.1.table, bf16[64,384]{1,0:T(8,128)(2,1)} %slice.210.cond, ...), custom_call_target="tpu_custom_call", output_to_operand_aliasing={{0}: (8, {}), {1}: (9, {}), {2}: (10, {}), {3}: (11, {})} | custom-call | flops 7927234560 | bytes 58982400 | tf_op jit(solution)/shard_map/cond_slots/pallas_call | solution.py:458
  333.6 8.7 %late_slots.1 = (f32[10,384,384]{2,1,0:T(8,128)}, f32[10,384,384]{2,1,0:T(8,128)}, f32[10,384,384]{2,1,0:T(8,128)}, f32[10,384,384]{2,1,0:T(8,128)}) custom-call(s32[4,4]{1,0:T(4,128)} %pad_add_fusion.table, ...), custom_call_target="tpu_custom_call", output_to_operand_aliasing={{0}: (14, {}), {1}: (15, {}), {2}: (16, {}), {3}: (17, {})} | custom-call | flops 3170893824 | bytes 23592960 | tf_op jit(solution)/shard_map/late_slots/pallas_call | solution.py:458
  (245 shorter events, 118.2 us)
Async XLA Ops:
  1.3 55.0 %collective-permute-start = (bf16[2,384]{1,0:T(2,128)(2,1)S(1)}, bf16[2,384]{1,0:T(2,128)(2,1)S(1)}, u32[]{:S(2)}, u32[]{:S(2)}) collective-permute-start(bf16[2,384]{1,0:T(2,128)(2,1)S(1)} %fusion.34), channel_id=1, source_target_pairs={{0,1},{1,0},{2,3},{3,2},{4,5},{5,4},{6,7},{7,6},{8,9},{9,8},{10,11... | collective-permute-start | bytes 4616 | tf_op jit(solution)/shard_map/ppermute | solution.py:83
  11.1 47.7 %collective-permute-start.2 = (bf16[3,192,384]{2,1,0:T(8,128)(2,1)}, bf16[3,192,384]{2,1,0:T(8,128)(2,1)S(1)}, u32[]{:S(2)}, u32[]{:S(2)}) collective-permute-start(bf16[3,192,384]{2,1,0:T(8,128)(2,1)} %pick_blocks.4), channel_id=1, source_target_pairs={{0,1},{1,0},{2,3},{3,2},{4,5},{5,4},{6,7},{7,6},{8,9},{9,8},{10,11... | collective-permute-start | bytes 1327112 | tf_op jit(solution)/shard_map/ppermute | solution.py:83
  18.3 46.0 %collective-permute-start.4 = (bf16[9,192,384]{2,1,0:T(8,128)(2,1)}, bf16[9,192,384]{2,1,0:T(8,128)(2,1)S(1)}, u32[]{:S(2)}, u32[]{:S(2)}) collective-permute-start(bf16[9,192,384]{2,1,0:T(8,128)(2,1)} %pick_blocks.5), channel_id=1, source_target_pairs={{0,1},{1,0},{2,3},{3,2},{4,5},{5,4},{6,7},{7,6},{8,9},{9,8},{10,11... | collective-permute-start | bytes 3981320 | tf_op jit(solution)/shard_map/ppermute | solution.py:83
  64.6 23.2 %collective-permute-start.5 = (bf16[9,192,384]{2,1,0:T(8,128)(2,1)S(1)}, bf16[9,192,384]{2,1,0:T(8,128)(2,1)S(1)}, u32[]{:S(2)}, u32[]{:S(2)}) collective-permute-start(bf16[9,192,384]{2,1,0:T(8,128)(2,1)S(1)} %add.281.near), channel_id=1, source_target_pairs={{0,2},{1,3},{2,0},{3,1},{4,6},{5,7},{6,4},{7,5},{8,10},{9,11},{10,... | collective-permute-start | bytes 3981320 | tf_op jit(solution)/shard_map/ppermute | solution.py:83
  193.2 10.6 %collective-permute-start.7 = (bf16[2,2688]{1,0:T(2,128)(2,1)S(1)}, bf16[2,2688]{1,0:T(2,128)(2,1)S(1)}, u32[]{:S(2)}, u32[]{:S(2)}) collective-permute-start(bf16[2,2688]{1,0:T(2,128)(2,1)S(1)} %pad_maximum_fusion.12), channel_id=1, source_target_pairs={{0,16},{1,17},{2,18},{3,19},{4,20},{5,21},{6,22},{7,23},{8,24},{9,... | collective-permute-start | bytes 32264 | tf_op jit(solution)/shard_map/ppermute | solution.py:83
  195.8 9.6 %collective-permute-start.6 = (bf16[2,2688]{1,0:T(2,128)(2,1)S(1)}, bf16[2,2688]{1,0:T(2,128)(2,1)S(1)}, u32[]{:S(2)}, u32[]{:S(2)}) collective-permute-start(bf16[2,2688]{1,0:T(2,128)(2,1)S(1)} %pad_maximum_fusion.12), channel_id=1, source_target_pairs={{0,8},{1,9},{2,10},{3,11},{4,12},{5,13},{6,14},{7,15},{8,0},{9,1},... | collective-permute-start | bytes 32264 | tf_op jit(solution)/shard_map/ppermute | solution.py:83
  199.2 27.6 %collective-permute-start.28 = (f32[1536,384]{1,0:T(8,128)}, f32[1536,384]{1,0:T(8,128)S(1)}, u32[]{:S(2)}, u32[]{:S(2)}) collective-permute-start(f32[1536,384]{1,0:T(8,128)} %dynamic-slice_bitcast_fusion), channel_id=1, source_target_pairs={{0,2},{1,3},{2,0},{3,1},{4,6},{5,7},{6,4},{7,5},{8,10},{9,11},{10,... | collective-permute-start | bytes 7077896 | tf_op jit(solution)/shard_map/ppermute | solution.py:83
  203.4 29.2 %collective-permute-start.14 = (f32[768,384]{1,0:T(8,128)}, f32[768,384]{1,0:T(8,128)}, u32[]{:S(2)}, u32[]{:S(2)}) collective-permute-start(f32[768,384]{1,0:T(8,128)} %dynamic-slice_bitcast_fusion.1), channel_id=1, source_target_pairs={{0,2},{1,3},{2,0},{3,1},{4,6},{5,7},{6,4},{7,5},{8,10},{9,11},{10,... | collective-permute-start | bytes 3538952 | tf_op jit(solution)/shard_map/ppermute | solution.py:83
  229.1 9.9 %collective-permute-start.29 = (bf16[384,384]{1,0:T(8,128)(2,1)S(1)}, bf16[384,384]{1,0:T(8,128)(2,1)S(1)}, u32[]{:S(2)}, u32[]{:S(2)}) collective-permute-start(bf16[384,384]{1,0:T(8,128)(2,1)S(1)} %get-tuple-element.191), channel_id=1, source_target_pairs={{0,4},{1,5},{2,6},{3,7},{4,0},{5,1},{6,2},{7,3},{8,12},{9,13},{10,... | collective-permute-start | bytes 884744 | tf_op jit(solution)/shard_map/ppermute | solution.py:83
  230.6 14.7 %collective-permute-start.31 = (bf16[384,384]{1,0:T(8,128)(2,1)S(1)}, bf16[384,384]{1,0:T(8,128)(2,1)S(1)}, u32[]{:S(2)}, u32[]{:S(2)}) collective-permute-start(bf16[384,384]{1,0:T(8,128)(2,1)S(1)} %get-tuple-element.192), channel_id=1, source_target_pairs={{0,5},{1,4},{2,7},{3,6},{4,1},{5,0},{6,3},{7,2},{8,13},{9,12},{10,... | collective-permute-start | bytes 884744 | tf_op jit(solution)/shard_map/ppermute | solution.py:83
  231.2 16.5 %collective-permute-start.30 = (bf16[384,384]{1,0:T(8,128)(2,1)S(1)}, bf16[384,384]{1,0:T(8,128)(2,1)S(1)}, u32[]{:S(2)}, u32[]{:S(2)}) collective-permute-start(bf16[384,384]{1,0:T(8,128)(2,1)S(1)} %get-tuple-element.193), channel_id=1, source_target_pairs={{0,1},{1,0},{2,3},{3,2},{4,5},{5,4},{6,7},{7,6},{8,9},{9,8},{10,11... | collective-permute-start | bytes 884744 | tf_op jit(solution)/shard_map/ppermute | solution.py:83
  234.1 16.1 %collective-permute-start.15 = (bf16[192,384]{1,0:T(8,128)(2,1)S(1)}, bf16[192,384]{1,0:T(8,128)(2,1)S(1)}, u32[]{:S(2)}, u32[]{:S(2)}) collective-permute-start(bf16[192,384]{1,0:T(8,128)(2,1)S(1)} %get-tuple-element.196), channel_id=1, source_target_pairs={{0,4},{1,5},{2,6},{3,7},{4,0},{5,1},{6,2},{7,3},{8,12},{9,13},{10,... | collective-permute-start | bytes 442376 | tf_op jit(solution)/shard_map/ppermute | solution.py:83
  235.7 16.6 %collective-permute-start.17 = (bf16[192,384]{1,0:T(8,128)(2,1)S(1)}, bf16[192,384]{1,0:T(8,128)(2,1)S(1)}, u32[]{:S(2)}, u32[]{:S(2)}) collective-permute-start(bf16[192,384]{1,0:T(8,128)(2,1)S(1)} %get-tuple-element.197), channel_id=1, source_target_pairs={{0,5},{1,4},{2,7},{3,6},{4,1},{5,0},{6,3},{7,2},{8,13},{9,12},{10,... | collective-permute-start | bytes 442376 | tf_op jit(solution)/shard_map/ppermute | solution.py:83
  239.0 13.3 %collective-permute-start.16 = (bf16[192,384]{1,0:T(8,128)(2,1)S(1)}, bf16[192,384]{1,0:T(8,128)(2,1)S(1)}, u32[]{:S(2)}, u32[]{:S(2)}) collective-permute-start(bf16[192,384]{1,0:T(8,128)(2,1)S(1)} %get-tuple-element.198), channel_id=1, source_target_pairs={{0,1},{1,0},{2,3},{3,2},{4,5},{5,4},{6,7},{7,6},{8,9},{9,8},{10,11... | collective-permute-start | bytes 442376 | tf_op jit(solution)/shard_map/ppermute | solution.py:83
  250.3 15.2 %collective-permute-start.33 = (f32[96,384]{1,0:T(8,128)S(1)}, f32[96,384]{1,0:T(8,128)S(1)}, u32[]{:S(2)}, u32[]{:S(2)}) collective-permute-start(f32[96,384]{1,0:T(8,128)S(1)} %get-tuple-element.200), channel_id=1, source_target_pairs={{0,16},{1,17},{2,18},{3,19},{4,20},{5,21},{6,22},{7,23},{8,24},{9,... | collective-permute-start | bytes 442376 | tf_op jit(solution)/shard_map/ppermute | solution.py:83
  250.3 15.2 %collective-permute-start.32 = (f32[96,384]{1,0:T(8,128)S(1)}, f32[96,384]{1,0:T(8,128)S(1)}, u32[]{:S(2)}, u32[]{:S(2)}) collective-permute-start(f32[96,384]{1,0:T(8,128)S(1)} %get-tuple-element.201), channel_id=1, source_target_pairs={{0,8},{1,9},{2,10},{3,11},{4,12},{5,13},{6,14},{7,15},{8,0},{9,1},... | collective-permute-start | bytes 442376 | tf_op jit(solution)/shard_map/ppermute | solution.py:83
  252.4 16.1 %collective-permute-start.20 = (f32[48,384]{1,0:T(8,128)S(1)}, f32[48,384]{1,0:T(8,128)S(1)}, u32[]{:S(2)}, u32[]{:S(2)}) collective-permute-start(f32[48,384]{1,0:T(8,128)S(1)} %get-tuple-element.208), channel_id=1, source_target_pairs={{0,24},{1,25},{2,26},{3,27},{4,28},{5,29},{6,30},{7,31},{8,16},{9,... | collective-permute-start | bytes 221192 | tf_op jit(solution)/shard_map/ppermute | solution.py:83
  254.8 15.1 %collective-permute-start.19 = (f32[48,384]{1,0:T(8,128)S(1)}, f32[48,384]{1,0:T(8,128)S(1)}, u32[]{:S(2)}, u32[]{:S(2)}) collective-permute-start(f32[48,384]{1,0:T(8,128)S(1)} %get-tuple-element.209), channel_id=1, source_target_pairs={{0,16},{1,17},{2,18},{3,19},{4,20},{5,21},{6,22},{7,23},{8,24},{9,... | collective-permute-start | bytes 221192 | tf_op jit(solution)/shard_map/ppermute | solution.py:83
  255.1 14.9 %collective-permute-start.18 = (f32[48,384]{1,0:T(8,128)S(1)}, f32[48,384]{1,0:T(8,128)S(1)}, u32[]{:S(2)}, u32[]{:S(2)}) collective-permute-start(f32[48,384]{1,0:T(8,128)S(1)} %get-tuple-element.210), channel_id=1, source_target_pairs={{0,8},{1,9},{2,10},{3,11},{4,12},{5,13},{6,14},{7,15},{8,0},{9,1},... | collective-permute-start | bytes 221192 | tf_op jit(solution)/shard_map/ppermute | solution.py:83
  274.5 11.2 %collective-permute-start.39 = (bf16[4,96,384]{2,1,0:T(8,128)(2,1)S(1)}, bf16[4,96,384]{2,1,0:T(8,128)(2,1)S(1)}, u32[]{:S(2)}, u32[]{:S(2)}) collective-permute-start(bf16[4,96,384]{2,1,0:T(8,128)(2,1)S(1)} %get-tuple-element.207), channel_id=1, source_target_pairs={{0,1},{1,0},{2,3},{3,2},{4,5},{5,4},{6,7},{7,6},{8,9},{9,8},{10,11... | collective-permute-start | bytes 884744 | tf_op jit(solution)/shard_map/ppermute | solution.py:83
  275.8 11.1 %collective-permute-start.38 = (bf16[4,96,384]{2,1,0:T(8,128)(2,1)S(1)}, bf16[4,96,384]{2,1,0:T(8,128)(2,1)S(1)}, u32[]{:S(2)}, u32[]{:S(2)}) collective-permute-start(bf16[4,96,384]{2,1,0:T(8,128)(2,1)S(1)} %get-tuple-element.207), channel_id=1, source_target_pairs={{0,4},{1,5},{2,6},{3,7},{4,0},{5,1},{6,2},{7,3},{8,12},{9,13},{10,... | collective-permute-start | bytes 884744 | tf_op jit(solution)/shard_map/ppermute | solution.py:83
  278.2 10.9 %collective-permute-start.40 = (bf16[4,96,384]{2,1,0:T(8,128)(2,1)S(1)}, bf16[4,96,384]{2,1,0:T(8,128)(2,1)S(1)}, u32[]{:S(2)}, u32[]{:S(2)}) collective-permute-start(bf16[4,96,384]{2,1,0:T(8,128)(2,1)S(1)} %get-tuple-element.207), channel_id=1, source_target_pairs={{0,5},{1,4},{2,7},{3,6},{4,1},{5,0},{6,3},{7,2},{8,13},{9,12},{10,... | collective-permute-start | bytes 884744 | tf_op jit(solution)/shard_map/ppermute | solution.py:83
  279.6 12.7 %collective-permute-start.25 = (bf16[4,48,384]{2,1,0:T(8,128)(2,1)S(1)}, bf16[4,48,384]{2,1,0:T(8,128)(2,1)S(1)}, u32[]{:S(2)}, u32[]{:S(2)}) collective-permute-start(bf16[4,48,384]{2,1,0:T(8,128)(2,1)S(1)} %get-tuple-element.212), channel_id=1, source_target_pairs={{0,1},{1,0},{2,3},{3,2},{4,5},{5,4},{6,7},{7,6},{8,9},{9,8},{10,11... | collective-permute-start | bytes 442376 | tf_op jit(solution)/shard_map/ppermute | solution.py:83
  280.3 11.9 %collective-permute-start.24 = (bf16[4,48,384]{2,1,0:T(8,128)(2,1)S(1)}, bf16[4,48,384]{2,1,0:T(8,128)(2,1)S(1)}, u32[]{:S(2)}, u32[]{:S(2)}) collective-permute-start(bf16[4,48,384]{2,1,0:T(8,128)(2,1)S(1)} %get-tuple-element.212), channel_id=1, source_target_pairs={{0,4},{1,5},{2,6},{3,7},{4,0},{5,1},{6,2},{7,3},{8,12},{9,13},{10,... | collective-permute-start | bytes 442376 | tf_op jit(solution)/shard_map/ppermute | solution.py:83
  (44 other events, 298.1 us)
